TPU v7x, 128 devices: a whole 4x4x4 slice. The times are simulated.
128 devices in a mesh: row: 16 (over x, y), col: 8 (over z, core).
Axes of the slice: x: 4, y: 4, z: 4, core: 2. Of those that a mesh axis runs over, the one named last changes fastest.
Arguments:
- object_slab: float32 [4, 4096, 4096], P(None, 'row', 'col'), may hold values from -6 to 6
- probe_wave: float32 [2, 256, 256], replicated, may hold values from -6 to 6
- scan_offsets: int32 [1024, 2], P(('row', 'col')), may hold values from 0 to 3840, as said below
- live_counts: int32 [128], P(('row', 'col')), may hold values from 1 to 8, as said below
- amplitudes: float32 [1024, 256, 256], P(('row', 'col')), may hold values from 0 to 3
Outputs:
- object_grad: float32 [4, 4096, 4096], P(None, 'row', 'col')
- probe_grad: float32 [2, 256, 256], replicated
Inputs may be any that keep to these rules, and one draw needn't show every extreme that they name: `scan_offsets`: each slot's window lies inside the object, and its corner lies in the object tile of the device that holds the slot. Slot 0 of the first device has corner (0, 0), slot 0 of the last device has corner (3840, 3840). `live_counts`: every device has at least one live slot and some device has all 8 slots live.
All inputs are finite; a program needn't handle non-finite values.
Results may differ from a plain program's by a relative error of at most 0.0003.
Values sent between devices are 32-bit elements; how exact they have to be, the bound alone decides.
No kernel may reach another device: no remote copies, remote signals or barrier semaphores. Data moves between devices by JAX's collectives and lax.ppermute only.
A program may use at most 128 MiB of HBM per device.

v0:
```python
import math

import jax
import jax.numpy as jnp
import ml_dtypes
import numpy as np
from jax import lax
from jax.experimental import pallas as pl
from jax.experimental.pallas import tpu as pltpu
from jax.sharding import PartitionSpec as P

W = 256
HALF_W = 128
TC = 512
EXT = TC + W
SLOTS = 8
GROUP = 4
PREPARED = 2
CHUNK = 32
F32 = jnp.float32
BF16 = jnp.bfloat16

RE, IM, NEG_IM = 0, 1, 2


def split_host(table):
    high = table.astype(np.float32).astype(ml_dtypes.bfloat16)
    low = (table - high.astype(np.float64)).astype(np.float32).astype(ml_dtypes.bfloat16)
    return [high, low]


def hop_tables():
    index = np.arange(W)
    dft = np.exp(-2j * np.pi / W * (index[:, None] * index[None, :] % W)) / math.sqrt(W)
    freqs = np.where(index < W // 2, index, index - W) / W
    fresnel = np.exp(-1j * np.pi * (W / 4.0) * freqs**2)
    hop = np.conj(dft) @ (fresnel[:, None] * dft)
    hop = hop * np.exp(1j * np.pi * index / W)
    out = []
    for table in (hop, hop.T):
        for part in (table.real, table.imag, -table.imag):
            out.extend(split_host(part))
    return np.stack(out)


def dft_tables():
    index = np.arange(W)
    angles = 2.0 * np.pi / W * (index[:, None] + 0.5) * (index[None, :HALF_W] + 0.5)
    table = np.concatenate([np.cos(angles), np.sin(angles)], axis=1) / math.sqrt(W)
    return np.stack(split_host(table) + split_host(table.T))


def fold_tables():
    source = np.concatenate([np.arange(HALF_W), np.arange(W - 1, HALF_W - 1, -1)])
    table = np.zeros((W, W), np.float32)
    table[source, np.arange(W)] = 1.0
    return np.stack([table, table.T]).astype(ml_dtypes.bfloat16)


def split(x):
    high = x.astype(BF16)
    return high, (x - high.astype(F32)).astype(BF16)


def lanes(*parts):
    return jnp.concatenate(parts, axis=1)


def rows(*parts):
    return jnp.concatenate(parts, axis=0)


def dot(a, b):
    return jnp.dot(a, b, preferred_element_type=F32)


def half_right(field, tab, at):
    high, low = tab[2 * at], tab[2 * at + 1]
    rh, rl = split(field[0])
    ih, il = split(field[1])
    out = dot(rows(lanes(rh, rl, rh), lanes(ih, il, ih)), rows(high, high, low))
    return out[:W], out[W:]


def half_left(field, tab, at):
    high, low = tab[2 * at], tab[2 * at + 1]
    rh, rl = split(field[0])
    ih, il = split(field[1])
    out = dot(lanes(high, high, low), lanes(rows(rh, rl, rh), rows(ih, il, ih)))
    return out[:, :W], out[:, W:]


def hop_parts(tab, at, conj):
    im, neg = (IM, NEG_IM) if not conj else (NEG_IM, IM)

    def three(a, b):
        a, b = 2 * (3 * at + a), 2 * (3 * at + b)
        return [tab[a], tab[b], tab[a], tab[b], tab[a + 1], tab[b + 1]]

    return three(RE, neg), three(im, RE)


def hop_right(field, tab, at, conj):
    rh, rl = split(field[0])
    ih, il = split(field[1])
    to_re, to_im = hop_parts(tab, at, conj)
    out = dot(lanes(rh, ih, rl, il, rh, ih), lanes(rows(*to_re), rows(*to_im)))
    return out[:, :W], out[:, W:]


def hop_left(field, tab, at, conj):
    rh, rl = split(field[0])
    ih, il = split(field[1])
    to_re, to_im = hop_parts(tab, at, conj)
    out = dot(rows(lanes(*to_re), lanes(*to_im)), rows(rh, ih, rl, il, rh, ih))
    return out[:W], out[W:]


def spread_right(field):
    c, s = field[0][:, :HALF_W], field[0][:, HALF_W:]
    d, t = field[1][:, :HALF_W], field[1][:, HALF_W:]
    return lanes(c + t, t - c), lanes(d - s, -d - s)


def spread_left(field):
    c, s = field[0][:HALF_W], field[0][HALF_W:]
    d, t = field[1][:HALF_W], field[1][HALF_W:]
    return rows(c + t, t - c), rows(d - s, -d - s)


def gather_right(field):
    a, b = field[0][:, :HALF_W], field[0][:, HALF_W:]
    c, d = field[1][:, :HALF_W], field[1][:, HALF_W:]
    return lanes(a - b, -c - d), lanes(c - d, a + b)


def gather_left(field):
    a, b = field[0][:HALF_W], field[0][HALF_W:]
    c, d = field[1][:HALF_W], field[1][HALF_W:]
    return rows(a - b, -c - d), rows(c - d, a + b)


def times(a, b):
    return a[0] * b[0] - a[1] * b[1], a[0] * b[1] + a[1] * b[0]


def conj_times(a, b):
    return a[0] * b[0] + a[1] * b[1], a[0] * b[1] - a[1] * b[0]


def pair(ref, *at):
    return ref[(*at, 0)], ref[(*at, 1)]


def put(value, ref, *at):
    ref[(*at, 0)], ref[(*at, 1)] = value


def chunks(body):
    def step(i, carry):
        body(pl.multiple_of(i * CHUNK, CHUNK))
        return carry

    lax.fori_loop(0, W // CHUNK, step, 0)


def geometry(meta, slot):
    row, col = meta[1 + slot], meta[1 + SLOTS + slot]
    block = col // W
    first = pl.multiple_of(block * W, W)
    second = pl.multiple_of(block * W + W, W)
    return row, col - block * W, first, second


def masks(row, col, at):
    in_top = lax.broadcasted_iota(jnp.int32, (CHUNK, W), 0) + at >= row
    in_first = lax.broadcasted_iota(jnp.int32, (CHUNK, W), 1) >= col
    return in_top, in_first


def load_window(meta, slot, ext, planes, win, u):
    row, col, first, second = geometry(meta, slot)
    border = row // CHUNK

    def load(i, carry):
        here = pl.ds(pl.multiple_of(i * CHUNK, CHUNK), CHUNK)
        _, in_first = masks(row, col, 0)
        low = (i < border).astype(jnp.int32)
        for p in planes:
            win[u, p, here, :] = jnp.where(
                in_first, ext[low, p, here, pl.ds(first, W)], ext[low, p, here, pl.ds(second, W)]
            )
        return carry

    lax.fori_loop(0, W // CHUNK, load, 0, unroll=2)
    at = pl.multiple_of(border * CHUNK, CHUNK)
    here = pl.ds(at, CHUNK)
    in_top, in_first = masks(row, col, at)
    for p in planes:
        low = jnp.where(in_first, ext[1, p, here, pl.ds(first, W)], ext[1, p, here, pl.ds(second, W)])
        win[u, p, here, :] = jnp.where(in_top, win[u, p, here, :], low)


def add_window(meta, slot, win, u, planes, gext):
    row, col, first, second = geometry(meta, slot)
    border = row // CHUNK
    zero = jnp.zeros((CHUNK, W), F32)

    def add(i, carry):
        at = pl.multiple_of(i * CHUNK, CHUNK)
        here = pl.ds(at, CHUNK)
        in_top, in_first = masks(row, col, at)
        low = (i < border).astype(jnp.int32)
        keep = jnp.logical_or(in_top, i < border)
        for p in planes:
            value = jnp.where(keep, win[u, p, here, :], zero)
            gext[low, p, here, pl.ds(first, W)] += jnp.where(in_first, value, zero)
            gext[low, p, here, pl.ds(second, W)] += jnp.where(in_first, zero, value)
        return carry

    lax.fori_loop(0, W // CHUNK, add, 0, unroll=2)
    at = pl.multiple_of(border * CHUNK, CHUNK)
    here = pl.ds(at, CHUNK)
    in_top, in_first = masks(row, col, at)
    for p in planes:
        value = jnp.where(in_top, zero, win[u, p, here, :])
        gext[1, p, here, pl.ds(first, W)] += jnp.where(in_first, value, zero)
        gext[1, p, here, pl.ds(second, W)] += jnp.where(in_first, zero, value)


def turn_probe(meta, slot, twice, turned, u):
    row, col, _, _ = geometry(meta, slot)
    for p in range(2):
        here = pl.ds(W - row, W)
        turned[u, p] = pltpu.roll(lanes(twice[p, 0, here, :], twice[p, 1, here, :]), col, 1)


def add_probe(meta, slot, part, u, acc):
    row, col, _, _ = geometry(meta, slot)
    for p in range(2):
        here = pl.ds(W - row, W)
        value = pltpu.roll(part[u, p], W - col, 1)
        acc[p, 0, here, :] += value[:, :HALF_W]
        acc[p, 1, here, :] += value[:, HALF_W:]


def tile_copies(refs, ext, sems):
    own, right, down0, down1, corner = refs
    return [
        (own, ext.at[0, :, :, pl.ds(0, TC)], sems.at[0]),
        (right, ext.at[0, :, :, pl.ds(TC, W)], sems.at[1]),
        (down0, ext.at[1, :, :, pl.ds(0, W)], sems.at[2]),
        (down1, ext.at[1, :, :, pl.ds(W, W)], sems.at[3]),
        (corner, ext.at[1, :, :, pl.ds(TC, W)], sems.at[4]),
    ]


def start_copies(copies):
    copies = [pltpu.make_async_copy(*copy) for copy in copies]
    for copy in copies:
        copy.start()
    return copies


def wait_copies(copies):
    for copy in copies:
        copy.wait()


def prepare_kernel(meta, twice, amp, fold, amp_out, turned):
    step = pl.program_id(0)

    def fold_amplitudes(u):
        high = amp[u].astype(BF16)
        rest = amp[u] - high.astype(F32)
        mid = rest.astype(BF16)
        low = (rest - mid.astype(F32)).astype(BF16)
        right_way = dot(rows(high, mid, low), fold[0])
        out = dot(fold[1], lanes(*(right_way[i * W : (i + 1) * W].astype(BF16) for i in range(3))))
        amp_out[u] = out[:, :W] + out[:, W : 2 * W] + out[:, 2 * W :]

    for u in range(PREPARED):
        fold_amplitudes(u)
        turn_probe(meta, step * PREPARED + u, twice, turned, u)


def first_kernel(meta, own, right, down0, down1, corner, turned, tab, prop, ext, win, sems):
    step = pl.program_id(0)

    @pl.when(step == 0)
    def begin():
        refs = (own.at[pl.ds(0, 2)], right.at[pl.ds(0, 2)], down0, down1, corner)
        wait_copies(start_copies(tile_copies(refs, ext, sems)))

    @pl.when(step * GROUP < meta[0])
    def work():
        for u in range(GROUP):
            load_window(meta, step * GROUP + u, ext, (0, 1), win, u)
        fields = [times(pair(turned, u), pair(win, u)) for u in range(GROUP)]
        fields = [hop_right(f, tab, 0, False) for f in fields]
        fields = [hop_left(f, tab, 1, False) for f in fields]
        for u, f in enumerate(fields):
            put(f, prop, u)


def second_kernel(meta, own, right, down0_one, down0_two, down1_one, down1_two, corner_one, corner_two, turned_in, hop_in,
                  prop, amp, dft, gown0, gown1, gright, gdown0, gdown1, gcorner, gprobe,
                  ext, gext, acc, turned, hop, win, sems):
    step = pl.program_id(0)
    group = range(GROUP)
    one, two = pl.ds(0, 2), pl.ds(2, 2)
    refs_one = (own.at[one], right.at[one], down0_one, down1_one, corner_one)
    refs_two = (own.at[two], right.at[two], down0_two, down1_two, corner_two)
    copies_one = tile_copies(refs_one, ext.at[:, one], sems.at[0])
    copies_two = tile_copies(refs_two, ext.at[:, two], sems.at[1])
    copy_turned = (turned_in, turned, sems.at[2, 0])
    copy_hop = (hop_in, hop, sems.at[2, 1])

    @pl.when(step == 0)
    def begin():
        started = start_copies(copies_two)
        start_copies([copy_hop] + copies_one + [copy_turned])
        gext[...] = jnp.zeros_like(gext)
        acc[...] = jnp.zeros_like(acc)
        wait_copies(started)

    live = step * GROUP < meta[0]

    @pl.when(live)
    def stage_one():
        for u in group:
            load_window(meta, step * GROUP + u, ext, (2, 3), win, u)
        fields = [times(pair(prop, u), (win[u, 2], win[u, 3])) for u in group]
        fields = [spread_left(half_left(f, dft, 1)) for f in fields]
        fields = [spread_right(half_right(f, dft, 0)) for f in fields]
        chi = []
        for u, f in enumerate(fields):
            factor = 1.0 - amp[u] * lax.rsqrt(f[0] * f[0] + f[1] * f[1] + 1.0)
            chi.append((factor * f[0], factor * f[1]))
        fields = [half_right(gather_right(f), dft, 1) for f in chi]
        fields = [half_left(gather_left(f), dft, 0) for f in fields]
        waves = [conj_times((win[u, 2], win[u, 3]), f) for u, f in enumerate(fields)]
        for u, f in enumerate(fields):
            win[u, 2], win[u, 3] = conj_times(pair(prop, u), f)
        for u, f in enumerate(waves):
            put(f, prop, u)

    @pl.when(step == 0)
    def arrive():
        wait_copies([pltpu.make_async_copy(*copy) for copy in [copy_hop] + copies_one + [copy_turned]])

    @pl.when(live)
    def stage_two():
        for u in group:
            load_window(meta, step * GROUP + u, ext, (0, 1), win, u)
        waves = [hop_left(pair(prop, u), hop, 0, True) for u in group]
        waves = [hop_right(f, hop, 1, True) for f in waves]
        for u, wave in enumerate(waves):
            probe = pair(turned, step * GROUP + u)
            grad, part = conj_times(probe, wave), conj_times(pair(win, u), wave)
            put(grad, win, u)
            put(part, prop, u)

        def finish(slot, u):
            add_window(meta, slot, win, u, range(4), gext)
            add_probe(meta, slot, prop, u, acc)

        for u in group:
            slot = step * GROUP + u
            pl.when(slot < meta[0])(lambda: finish(slot, u))

    @pl.when(step == SLOTS // GROUP - 1)
    def end():
        sem = sems.at[0]
        outs = start_copies([
            (gext.at[1, :, :, pl.ds(W, W)], gdown1, sem.at[0]),
            (gext.at[1, :, :, pl.ds(TC, W)], gcorner, sem.at[1]),
            (gext.at[1, :, :, pl.ds(0, W)], gdown0, sem.at[2]),
            (gext.at[0, :, :, pl.ds(TC, W)], gright, sem.at[3]),
            (gext.at[0, :, :, pl.ds(0, W)], gown0, sem.at[4]),
            (gext.at[0, :, :, pl.ds(W, W)], gown1, sems.at[1, 0]),
        ])
        for p in range(2):
            gprobe[p] = lanes(acc[p, 0, :W, :] + acc[p, 0, W:, :], acc[p, 1, :W, :] + acc[p, 1, W:, :])
        wait_copies(outs)


ANYWHERE = pl.BlockSpec(memory_space=pl.ANY)
WHOLE = pl.BlockSpec(memory_space=pltpu.VMEM)
SCALARS = pl.BlockSpec(memory_space=pltpu.SMEM)
FIELDS = pl.BlockSpec((GROUP, 2, W, W), lambda i: (i, 0, 0, 0))
PLANES = pl.BlockSpec((GROUP, W, W), lambda i: (i, 0, 0))


def shape(*dims):
    return jax.ShapeDtypeStruct(dims, F32)


FIELDS_SHAPE = shape(SLOTS, 2, W, W)


def call(kernel, steps, in_specs, out_specs, out_shape, scratch, products):
    return pl.pallas_call(
        kernel,
        grid=(steps,),
        in_specs=in_specs,
        out_specs=out_specs,
        out_shape=out_shape,
        scratch_shapes=scratch,
        compiler_params=pltpu.CompilerParams(
            vmem_limit_bytes=56 * 2**20, dimension_semantics=("arbitrary",)
        ),
        cost_estimate=pl.CostEstimate(
            flops=SLOTS * products * 2 * W**3, bytes_accessed=12 * 2**20, transcendentals=0
        ),
    )


def prepare_call(*args):
    return call(
        prepare_kernel,
        SLOTS // PREPARED,
        [SCALARS, WHOLE, pl.BlockSpec((PREPARED, W, W), lambda i: (i, 0, 0)), WHOLE],
        [
            pl.BlockSpec((PREPARED, W, W), lambda i: (i, 0, 0)),
            pl.BlockSpec((PREPARED, 2, W, W), lambda i: (i, 0, 0, 0)),
        ],
        [shape(SLOTS, W, W), FIELDS_SHAPE],
        [],
        6,
    )(*args)


def first_call(*args):
    return call(
        first_kernel,
        SLOTS // GROUP,
        [SCALARS] + [ANYWHERE] * 5 + [FIELDS, WHOLE],
        FIELDS,
        FIELDS_SHAPE,
        [
            pltpu.VMEM((2, 2, W, EXT), F32),
            pltpu.VMEM((GROUP, 2, W, W), F32),
            pltpu.SemaphoreType.DMA((5,)),
        ],
        24,
    )(*args)


def second_call(*args):
    return call(
        second_kernel,
        SLOTS // GROUP,
        [SCALARS] + [ANYWHERE] * 10 + [FIELDS, PLANES, WHOLE],
        [ANYWHERE] * 6 + [WHOLE],
        [shape(4, W, W)] * 6 + [shape(2, W, W)],
        [
            pltpu.VMEM((2, 4, W, EXT), F32),
            pltpu.VMEM((2, 4, W, EXT), F32),
            pltpu.VMEM((2, 2, 2 * W, HALF_W), F32),
            pltpu.VMEM((SLOTS, 2, W, W), F32),
            pltpu.VMEM((12, W, W), BF16),
            pltpu.VMEM((GROUP, 4, W, W), F32),
            pltpu.SemaphoreType.DMA((3, 5)),
        ],
        48,
    )(*args)


def shift(value, axis, steps):
    count = lax.axis_size(axis)
    first, last = (max(0, -steps), min(count, count - steps))
    return lax.ppermute(value, axis, [(source, source + steps) for source in range(first, last)])


def add_shares(value, axis):
    count = lax.axis_size(axis)
    shares = value.reshape(count, -1, value.shape[-1])
    return lax.all_to_all(shares, axis, 0, 0, tiled=True).sum(axis=0)


def hand_out(value, axis):
    spread = jnp.broadcast_to(value[None], (lax.axis_size(axis), *value.shape))
    return lax.all_to_all(spread, axis, 0, 0, tiled=True)


def probe_twice(probe):
    halves = probe.reshape(2, W, 2, HALF_W).transpose(0, 2, 1, 3)
    return jnp.concatenate([halves, halves], axis=2)


def body(object_slab, probe_wave, scan_offsets, live_counts, amplitudes):
    rows_tile, cols_tile = object_slab.shape[1:]
    local_rows = scan_offsets[:, 0] - lax.axis_index("row") * rows_tile
    local_cols = scan_offsets[:, 1] - lax.axis_index("col") * cols_tile
    meta = jnp.concatenate([live_counts, local_rows, local_cols])
    hop, dft, fold = jnp.asarray(hop_tables()), jnp.asarray(dft_tables()), jnp.asarray(fold_tables())
    twice = probe_twice(probe_wave)
    down0_one = shift(object_slab[:2, :, :W], "row", -1)
    down1_one = shift(object_slab[:2, :, W:], "row", -1)
    right = shift(object_slab[:, :, :W], "col", -1)
    down0_two = shift(object_slab[2:, :, :W], "row", -1)
    down0_one, last_part = lax.optimization_barrier((down0_one, object_slab[2:, :, W:]))
    down1_two = shift(last_part, "row", -1)
    corner_one = shift(down0_one, "col", -1)
    amp, turned = prepare_call(meta, twice, amplitudes, fold)
    prop = first_call(meta, object_slab, right, down0_one, down1_one, corner_one, turned, hop)
    down0_two, prop = lax.optimization_barrier((down0_two, prop))
    corner_two = shift(down0_two, "col", -1)
    gown0, gown1, gright, gdown0, gdown1, gcorner, gprobe = second_call(
        meta, object_slab, right, down0_one, down0_two, down1_one, down1_two, corner_one, corner_two, turned, hop,
        prop, amp, dft,
    )
    corner_back = shift(gcorner, "col", 1)
    down1_back = shift(gdown1, "row", 1)
    share = add_shares(gprobe, "row")
    gdown0, gright, share = lax.optimization_barrier((gdown0 + corner_back, gright, share))
    down0_back = shift(gdown0, "row", 1)
    right_back = shift(gright, "col", 1)
    share = hand_out(share, "col").sum(axis=0)
    own0, own1 = lax.optimization_barrier((gown0 + right_back, gown1 + down1_back))
    probe_grad = hand_out(share, "row").reshape(probe_wave.shape)
    object_grad = jnp.concatenate([own0 + down0_back, own1], axis=2)
    return object_grad, probe_grad


def solution(mesh):
    return jax.shard_map(
        body,
        mesh=mesh,
        in_specs=(
            P(None, "row", "col"),
            P(),
            P(("row", "col"), None),
            P(("row", "col")),
            P(("row", "col"), None, None),
        ),
        out_specs=(P(None, "row", "col"), P()),
        check_vma=False,
    )
```

profile of v0, /device:TPU:6, one launch (start us, length us, event | category | flops | bytes accessed | tf_op | source)
XLA Modules:
  0.0 180.9 jit_solution(154457478701041764)
XLA Ops:
  0.6 0.0 copy-start
  0.6 2.8 %fusion = (f32[2,256,256]{2,1,0:T(8,128)}, f32[2,256,256]{2,1,0:T(8,128)S(1)}, f32[2,256,256]{2,1,0:T(8,128)S(1)}, f32[2,256,256]{2,1,0:T(8,128)}) fusion(f32[4,256,512]{2,1,0:T(8,128)} %own.3), kind=kLoop, calls=%fused_computation.5 | loop fusion | bytes 4194304 | tf_op jit(solution)/shard_map/slice | solution.py:500
  3.5 0.0 copy-start.4
  3.5 0.0 copy-start.5
  3.5 5.3 %collective-permute-start.1 = (f32[2,256,256]{2,1,0:T(8,128)}, f32[2,256,256]{2,1,0:T(8,128)}, u32[]{:S(2)}, u32[]{:S(2)}) collective-permute-start(f32[2,256,256]{2,1,0:T(8,128)} %get-tuple-element.41), channel_id=1, source_target_pairs={{8,0},{16,8},{24,16},{32,24},{40,32},{48,40},{56,48},{64,56},{72,6... | collective-permute-start | bytes 1572872 | tf_op jit(solution)/shard_map/ppermute | solution.py:473
  8.8 0.0 copy-done
  8.8 0.1 slice.23
  8.9 1.3 collective-permute-start
  10.2 2.7 %collective-permute-start.3 = (f32[2,256,256]{2,1,0:T(8,128)}, f32[2,256,256]{2,1,0:T(8,128)}, u32[]{:S(2)}, u32[]{:S(2)}) collective-permute-start(f32[2,256,256]{2,1,0:T(8,128)} %get-tuple-element.38), channel_id=1, source_target_pairs={{8,0},{16,8},{24,16},{32,24},{40,32},{48,40},{56,48},{64,56},{72,6... | collective-permute-start | bytes 1572872 | tf_op jit(solution)/shard_map/ppermute | solution.py:473
  12.9 2.4 %collective-permute-start.2 = (f32[2,256,256]{2,1,0:T(8,128)S(1)}, f32[2,256,256]{2,1,0:T(8,128)}, u32[]{:S(2)}, u32[]{:S(2)}) collective-permute-start(f32[2,256,256]{2,1,0:T(8,128)S(1)} %get-tuple-element.39), channel_id=1, source_target_pairs={{8,0},{16,8},{24,16},{32,24},{40,32},{48,40},{56,48},{64,56},{72,6... | collective-permute-start | bytes 1572872 | tf_op jit(solution)/shard_map/ppermute | solution.py:473
  15.9 0.0 copy-done.4
  15.9 0.2 copy.12
  16.1 0.2 copy.13
  16.3 5.1 %collective-permute-done.1.down0.down0_one = f32[2,256,256]{2,1,0:T(8,128)} collective-permute-done((f32[2,256,256]{2,1,0:T(8,128)}, f32[2,256,256]{2,1,0:T(8,128)}, u32[]{:S(2)}, u32[]{:S(2)}) %collective-permute-start.1) | collective-permute-done | bytes 524320 | tf_op jit(solution)/shard_map/ppermute | solution.py:473
  21.4 1.3 collective-permute-start.4
  22.7 0.0 copy-done.5
  22.7 0.6 pad_add_fusion.meta
  23.3 1.1 pad_maximum_fusion.1.twice
  24.4 6.3 %shard_map.95 = (f32[8,256,256]{2,1,0:T(8,128)}, f32[8,2,256,256]{3,2,1,0:T(8,128)}) custom-call(s32[17]{0:T(128)} %pad_add_fusion.meta, f32[2,2,512,128]{3,2,1,0:T(8,128)} %pad_maximum_fusion.1.twice, f32[8,256,256]{2,1,0:T(8,128)} %amp.1, bf16[2,256,256]{2,1,0:T(8,128)(2,1)} %constant.23.clone.fold), custom_call_target="tpu_custom_call" | custom-call | flops 1610612736 | bytes 12582912 | tf_op jit(solution)/shard_map/pallas_call | solution.py:420
  30.7 6.5 %collective-permute-start.5 = (f32[2,256,256]{2,1,0:T(8,128)S(1)}, f32[2,256,256]{2,1,0:T(8,128)S(1)}, u32[]{:S(2)}, u32[]{:S(2)}) collective-permute-start(f32[2,256,256]{2,1,0:T(8,128)S(1)} %get-tuple-element.23), channel_id=1, source_target_pairs={{8,0},{16,8},{24,16},{32,24},{40,32},{48,40},{56,48},{64,56},{72,6... | collective-permute-start | bytes 1572872 | tf_op jit(solution)/shard_map/ppermute | solution.py:473
  37.2 0.0 collective-permute-done.3.down1.down1_one
  37.2 0.0 collective-permute-done.right
  37.2 0.0 collective-permute-done.4.corner.corner_one
  37.2 0.0 copy-start.6
  37.3 0.8 copy-done.6
  38.0 13.2 %shard_map.96.prop = f32[8,2,256,256]{3,2,1,0:T(8,128)} custom-call(s32[17]{0:T(128)} %pad_add_fusion.meta, f32[4,256,512]{2,1,0:T(8,128)} %own.3, f32[4,256,256]{2,1,0:T(8,128)} %collective-permute-done.right, f32[2,256,256]{2,1,0:T(8,128)} %collective-permute-done.1.down0.down0_one, f32[2,256,256]{2,1,0:T(8,128)} %collective-permute-done.3.down1.down1_one, ...), custom_call_target="tpu_custom_call" | custom-call | flops 6442450944 | bytes 12582912 | tf_op jit(solution)/shard_map/pallas_call | solution.py:435
  51.3 0.0 collective-permute-done.2.down0_two
  51.3 1.5 collective-permute-start.6
  52.7 1.1 collective-permute-done.5.down1_two
  53.9 0.0 copy-start.7
  53.9 1.4 collective-permute-done.6.corner_two
  55.3 0.0 copy-start.8
  55.3 0.0 copy-done.7
  55.3 0.8 copy-done.8
  56.1 28.7 %shard_map.97 = (f32[4,256,256]{2,1,0:T(8,128)}, f32[4,256,256]{2,1,0:T(8,128)}, f32[4,256,256]{2,1,0:T(8,128)}, f32[4,256,256]{2,1,0:T(8,128)}, f32[4,256,256]{...) custom-call(s32[17]{0:T(128)} %pad_add_fusion.meta, f32[4,256,512]{2,1,0:T(8,128)} %own.3, ...), custom_call_target="tpu_custom_call" | custom-call | flops 12884901888 | bytes 12582912 | tf_op jit(solution)/shard_map/pallas_call | solution.py:451
  84.8 0.0 copy-start.2
  84.8 2.5 %collective-permute-start.7 = (f32[4,256,256]{2,1,0:T(8,128)}, f32[4,256,256]{2,1,0:T(8,128)}, u32[]{:S(2)}, u32[]{:S(2)}) collective-permute-start(f32[4,256,256]{2,1,0:T(8,128)} %get-tuple-element.28), channel_id=1, source_target_pairs={{0,1},{1,2},{2,3},{3,4},{4,5},{5,6},{6,7},{8,9},{9,10},{10,11},{11... | collective-permute-start | bytes 3145736 | tf_op jit(solution)/shard_map/ppermute | solution.py:473
  87.2 7.3 %all-to-all-start = ((f32[16,32,256]{2,1,0:T(8,128)}), f32[16,32,256]{2,1,0:T(8,128)S(1)}, u32[]{:S(2)}, u32[]{:S(2)}) async-start(f32[16,32,256]{2,1,0:T(8,128)} %bitcast.11), calls=%async_computation | async-start | bytes 1048576 | tf_op jit(solution)/shard_map/all_to_all | solution.py:479
  94.6 3.4 %collective-permute-start.9 = (f32[4,256,256]{2,1,0:T(8,128)}, f32[4,256,256]{2,1,0:T(8,128)S(1)}, u32[]{:S(2)}, u32[]{:S(2)}) collective-permute-start(f32[4,256,256]{2,1,0:T(8,128)} %get-tuple-element.33), channel_id=1, source_target_pairs={{0,8},{8,16},{16,24},{24,32},{32,40},{40,48},{48,56},{56,64},{64,7... | collective-permute-start | bytes 3145736 | tf_op jit(solution)/shard_map/ppermute | solution.py:473
  97.9 6.7 %all-to-all-done = f32[16,32,256]{2,1,0:T(8,128)S(1)} async-done(((f32[16,32,256]{2,1,0:T(8,128)}), f32[16,32,256]{2,1,0:T(8,128)S(1)}, u32[]{:S(2)}, u32[]{:S(2)}) %all-to-all-start) | async-done | bytes 524320 | tf_op jit(solution)/shard_map/all_to_all | solution.py:479
  104.7 0.0 collective-permute-done.7
  104.7 0.0 copy-done.2
  104.7 2.4 %add.12 = f32[4,256,256]{2,1,0:T(8,128)} add(f32[4,256,256]{2,1,0:T(8,128)S(1)} %copy-done.2, f32[4,256,256]{2,1,0:T(8,128)} %collective-permute-done.7) | non-fusion elementwise | flops 262144 | bytes 3145728 | tf_op jit(solution)/shard_map/add | solution.py:517
  107.1 2.3 %collective-permute-start.8 = (f32[4,256,256]{2,1,0:T(8,128)}, f32[4,256,256]{2,1,0:T(8,128)}, u32[]{:S(2)}, u32[]{:S(2)}) collective-permute-start(f32[4,256,256]{2,1,0:T(8,128)} %get-tuple-element.31), channel_id=1, source_target_pairs={{0,1},{1,2},{2,3},{3,4},{4,5},{5,6},{6,7},{8,9},{9,10},{10,11},{11... | collective-permute-start | bytes 3145736 | tf_op jit(solution)/shard_map/ppermute | solution.py:473
  109.4 3.4 %collective-permute-start.10 = (f32[4,256,256]{2,1,0:T(8,128)}, f32[4,256,256]{2,1,0:T(8,128)}, u32[]{:S(2)}, u32[]{:S(2)}) collective-permute-start(f32[4,256,256]{2,1,0:T(8,128)} %add.12), channel_id=1, source_target_pairs={{0,8},{8,16},{16,24},{24,32},{32,40},{40,48},{48,56},{56,64},{64,7... | collective-permute-start | bytes 3145736 | tf_op jit(solution)/shard_map/ppermute | solution.py:473
  112.8 13.9 %all_to_all.15 = f32[8,32,256]{2,1,0:T(8,128)S(1)} all-to-all(f32[8,32,256]{2,1,0:T(8,128)S(1)} %broadcast_in_dim.4), channel_id=1, replica_groups=mesh['row'=16,'col'=8] {'col'}, dimensions={0} | all-to-all | bytes 524288 | tf_op jit(solution)/shard_map/all_to_all | solution.py:484
  126.7 0.8 broadcast_in_dim.5
  127.5 0.0 copy-start.1
  127.5 37.5 %all-to-all-start.2 = ((f32[16,32,256]{2,1,0:T(8,128)}), f32[16,32,256]{2,1,0:T(8,128)S(1)}, u32[]{:S(2)}, u32[]{:S(2)}) async-start(f32[16,32,256]{2,1,0:T(8,128)} %broadcast_in_dim.5), calls=%async_computation.2 | async-start | bytes 1048576 | tf_op jit(solution)/shard_map/all_to_all | solution.py:484
  165.1 0.0 collective-permute-done.9
  165.1 0.0 copy-start.3
  165.1 1.0 copy-done.3
  166.0 1.7 add.14
  167.7 8.0 %all-to-all-done.2 = f32[16,32,256]{2,1,0:T(8,128)S(1)} async-done(((f32[16,32,256]{2,1,0:T(8,128)}), f32[16,32,256]{2,1,0:T(8,128)S(1)}, u32[]{:S(2)}, u32[]{:S(2)}) %all-to-all-start.2) | async-done | bytes 524320 | tf_op jit(solution)/shard_map/all_to_all | solution.py:484
  175.7 0.0 collective-permute-done.8
  175.7 0.0 copy-done.1
  175.7 1.4 add.13
  177.1 0.0 collective-permute-done.10
  177.1 1.4 add.15
  178.5 1.6 pad_maximum_fusion
  180.1 0.8 copy.16
  (4 shorter events, 0.1 us)
Async XLA Ops:
  0.6 8.2 %copy-start = (f32[4,256,512]{2,1,0:T(8,128)S(1)}, f32[4,256,512]{2,1,0:T(8,128)}, u32[]{:S(2)}) copy-start(f32[4,256,512]{2,1,0:T(8,128)} %own.3) | copy-start | bytes 6291460
  3.5 12.4 %copy-start.4 = (f32[2,256,256]{2,1,0:T(8,128)S(1)}, f32[2,256,256]{2,1,0:T(8,128)}, u32[]{:S(2)}) copy-start(f32[2,256,256]{2,1,0:T(8,128)} %param.9) | copy-start | bytes 1572868
  3.5 19.2 %copy-start.5 = (s32[8,2]{0,1:T(2,128)S(1)}, s32[8,2]{0,1:T(2,128)}, u32[]{:S(2)}) copy-start(s32[8,2]{0,1:T(2,128)} %param.10) | copy-start | bytes 196
  3.5 17.9 %collective-permute-start.1 = (f32[2,256,256]{2,1,0:T(8,128)}, f32[2,256,256]{2,1,0:T(8,128)}, u32[]{:S(2)}, u32[]{:S(2)}) collective-permute-start(f32[2,256,256]{2,1,0:T(8,128)} %get-tuple-element.41), channel_id=1, source_target_pairs={{8,0},{16,8},{24,16},{32,24},{40,32},{48,40},{56,48},{64,56},{72,6... | collective-permute-start | bytes 1572872 | tf_op jit(solution)/shard_map/ppermute | solution.py:473
  8.9 28.3 %collective-permute-start = (f32[4,256,256]{2,1,0:T(8,128)S(1)}, f32[4,256,256]{2,1,0:T(8,128)}, u32[]{:S(2)}, u32[]{:S(2)}) collective-permute-start(f32[4,256,256]{2,1,0:T(8,128)S(1)} %slice.23), channel_id=1, source_target_pairs={{1,0},{2,1},{3,2},{4,3},{5,4},{6,5},{7,6},{9,8},{10,9},{11,10},{12... | collective-permute-start | bytes 3145736 | tf_op jit(solution)/shard_map/ppermute | solution.py:473
  10.2 27.0 %collective-permute-start.3 = (f32[2,256,256]{2,1,0:T(8,128)}, f32[2,256,256]{2,1,0:T(8,128)}, u32[]{:S(2)}, u32[]{:S(2)}) collective-permute-start(f32[2,256,256]{2,1,0:T(8,128)} %get-tuple-element.38), channel_id=1, source_target_pairs={{8,0},{16,8},{24,16},{32,24},{40,32},{48,40},{56,48},{64,56},{72,6... | collective-permute-start | bytes 1572872 | tf_op jit(solution)/shard_map/ppermute | solution.py:473
  12.9 38.4 %collective-permute-start.2 = (f32[2,256,256]{2,1,0:T(8,128)S(1)}, f32[2,256,256]{2,1,0:T(8,128)}, u32[]{:S(2)}, u32[]{:S(2)}) collective-permute-start(f32[2,256,256]{2,1,0:T(8,128)S(1)} %get-tuple-element.39), channel_id=1, source_target_pairs={{8,0},{16,8},{24,16},{32,24},{40,32},{48,40},{56,48},{64,56},{72,6... | collective-permute-start | bytes 1572872 | tf_op jit(solution)/shard_map/ppermute | solution.py:473
  21.4 15.8 %collective-permute-start.4 = (f32[2,256,256]{2,1,0:T(8,128)}, f32[2,256,256]{2,1,0:T(8,128)S(1)}, u32[]{:S(2)}, u32[]{:S(2)}) collective-permute-start(f32[2,256,256]{2,1,0:T(8,128)} %collective-permute-done.1.down0.down0_one), channel_id=1, source_target_pairs={{1,0},{2,1},{3,2},{4,3},{5,4},{6,5},{7,6},{9,8},{10,9},{11,10},{12... | collective-permute-start | bytes 1572872 | tf_op jit(solution)/shard_map/ppermute | solution.py:473
  30.7 23.1 %collective-permute-start.5 = (f32[2,256,256]{2,1,0:T(8,128)S(1)}, f32[2,256,256]{2,1,0:T(8,128)S(1)}, u32[]{:S(2)}, u32[]{:S(2)}) collective-permute-start(f32[2,256,256]{2,1,0:T(8,128)S(1)} %get-tuple-element.23), channel_id=1, source_target_pairs={{8,0},{16,8},{24,16},{32,24},{40,32},{48,40},{56,48},{64,56},{72,6... | collective-permute-start | bytes 1572872 | tf_op jit(solution)/shard_map/ppermute | solution.py:473
  37.2 0.8 copy-start.6
  51.3 4.0 %collective-permute-start.6 = (f32[2,256,256]{2,1,0:T(8,128)}, f32[2,256,256]{2,1,0:T(8,128)S(1)}, u32[]{:S(2)}, u32[]{:S(2)}) collective-permute-start(f32[2,256,256]{2,1,0:T(8,128)} %collective-permute-done.2.down0_two), channel_id=1, source_target_pairs={{1,0},{2,1},{3,2},{4,3},{5,4},{6,5},{7,6},{9,8},{10,9},{11,10},{12... | collective-permute-start | bytes 1572872 | tf_op jit(solution)/shard_map/ppermute | solution.py:473
  53.9 1.4 copy-start.7
  55.3 0.8 copy-start.8
  84.8 20.0 %copy-start.2 = (f32[4,256,256]{2,1,0:T(8,128)S(1)}, f32[4,256,256]{2,1,0:T(8,128)}, u32[]{:S(2)}) copy-start(f32[4,256,256]{2,1,0:T(8,128)} %get-tuple-element.27) | copy-start | bytes 3145732
  84.8 19.9 %collective-permute-start.7 = (f32[4,256,256]{2,1,0:T(8,128)}, f32[4,256,256]{2,1,0:T(8,128)}, u32[]{:S(2)}, u32[]{:S(2)}) collective-permute-start(f32[4,256,256]{2,1,0:T(8,128)} %get-tuple-element.28), channel_id=1, source_target_pairs={{0,1},{1,2},{2,3},{3,4},{4,5},{5,6},{6,7},{8,9},{9,10},{10,11},{11... | collective-permute-start | bytes 3145736 | tf_op jit(solution)/shard_map/ppermute | solution.py:473
  87.2 17.4 %all-to-all-start = ((f32[16,32,256]{2,1,0:T(8,128)}), f32[16,32,256]{2,1,0:T(8,128)S(1)}, u32[]{:S(2)}, u32[]{:S(2)}) async-start(f32[16,32,256]{2,1,0:T(8,128)} %bitcast.11), calls=%async_computation | async-start | bytes 1048576 | tf_op jit(solution)/shard_map/all_to_all | solution.py:479
  94.6 70.5 %collective-permute-start.9 = (f32[4,256,256]{2,1,0:T(8,128)}, f32[4,256,256]{2,1,0:T(8,128)S(1)}, u32[]{:S(2)}, u32[]{:S(2)}) collective-permute-start(f32[4,256,256]{2,1,0:T(8,128)} %get-tuple-element.33), channel_id=1, source_target_pairs={{0,8},{8,16},{16,24},{24,32},{32,40},{40,48},{48,56},{56,64},{64,7... | collective-permute-start | bytes 3145736 | tf_op jit(solution)/shard_map/ppermute | solution.py:473
  107.1 68.6 %collective-permute-start.8 = (f32[4,256,256]{2,1,0:T(8,128)}, f32[4,256,256]{2,1,0:T(8,128)}, u32[]{:S(2)}, u32[]{:S(2)}) collective-permute-start(f32[4,256,256]{2,1,0:T(8,128)} %get-tuple-element.31), channel_id=1, source_target_pairs={{0,1},{1,2},{2,3},{3,4},{4,5},{5,6},{6,7},{8,9},{9,10},{10,11},{11... | collective-permute-start | bytes 3145736 | tf_op jit(solution)/shard_map/ppermute | solution.py:473
  109.4 67.7 %collective-permute-start.10 = (f32[4,256,256]{2,1,0:T(8,128)}, f32[4,256,256]{2,1,0:T(8,128)}, u32[]{:S(2)}, u32[]{:S(2)}) collective-permute-start(f32[4,256,256]{2,1,0:T(8,128)} %add.12), channel_id=1, source_target_pairs={{0,8},{8,16},{16,24},{24,32},{32,40},{40,48},{48,56},{56,64},{64,7... | collective-permute-start | bytes 3145736 | tf_op jit(solution)/shard_map/ppermute | solution.py:473
  127.5 48.2 %copy-start.1 = (f32[4,256,256]{2,1,0:T(8,128)S(1)}, f32[4,256,256]{2,1,0:T(8,128)}, u32[]{:S(2)}) copy-start(f32[4,256,256]{2,1,0:T(8,128)} %get-tuple-element.26) | copy-start | bytes 3145732
  127.5 48.2 %all-to-all-start.2 = ((f32[16,32,256]{2,1,0:T(8,128)}), f32[16,32,256]{2,1,0:T(8,128)S(1)}, u32[]{:S(2)}, u32[]{:S(2)}) async-start(f32[16,32,256]{2,1,0:T(8,128)} %broadcast_in_dim.5), calls=%async_computation.2 | async-start | bytes 1048576 | tf_op jit(solution)/shard_map/all_to_all | solution.py:484
  165.1 1.0 copy-start.3
where the time goes:
time: 184 us; the launch traced here: 181 us
  starting transfers between devices  77.2 us (42%)
  Pallas kernels  48.2 us (26%)
  waiting for transfers between devices  22.4 us (12%)
  blocking collectives  13.9 us (8%)
  other arithmetic  10.1 us (5%)
  local copies, waits for them, and re-layouts  7.55 us (4%)
    all_to_all x1, starting transfers between devices, hand_out(): return lax.all_to_all(spread, axis, 0, 0, tiled=True)  37.5 us
    ppermute x11, starting transfers between devices, shift(): lax.ppermute(value, axis, [(source, source + steps) for source in range(f...  32.4 us
    pallas_call x1, Pallas kernels, second_call(): call(second_kernel, SLOTS // GROUP, [SCALARS] + [ANYWHERE] * 10 + [FIELDS...  28.7 us
    all_to_all x1, blocking collectives, hand_out(): return lax.all_to_all(spread, axis, 0, 0, tiled=True)  13.9 us
    pallas_call x1, Pallas kernels, first_call(): call(first_kernel, SLOTS // GROUP, [SCALARS] + [ANYWHERE] * 5 + [FIELDS,...  13.2 us
    all_to_all x1, waiting for transfers between devices, hand_out(): return lax.all_to_all(spread, axis, 0, 0, tiled=True)  7.99 us
    ppermute x11, waiting for transfers between devices, shift(): lax.ppermute(value, axis, [(source, source + steps) for source in range(f...  7.65 us
    all_to_all x1, starting transfers between devices, add_shares(): return lax.all_to_all(shares, axis, 0, 0, tiled=True).sum(axis=0)  7.33 us
  transfers between devices with their start and end apart: 13, of which 5 were waited for; matrix products, arithmetic and copies ran while one was open for 5% of the time, Pallas kernels for 11%

commit v1 on v0

--- a/solution.py
+++ b/solution.py
@@ -512,10 +512,10 @@
         prop, amp, dft,
     )
     corner_back = shift(gcorner, "col", 1)
+    share = add_shares(gprobe, "row")
+    gdown0, gdown1, gright, share = lax.optimization_barrier((gdown0, gdown1, gright, share))
     down1_back = shift(gdown1, "row", 1)
-    share = add_shares(gprobe, "row")
-    gdown0, gright, share = lax.optimization_barrier((gdown0 + corner_back, gright, share))
-    down0_back = shift(gdown0, "row", 1)
+    down0_back = shift(gdown0 + corner_back, "row", 1)
     right_back = shift(gright, "col", 1)
     share = hand_out(share, "col").sum(axis=0)
     own0, own1 = lax.optimization_barrier((gown0 + right_back, gown1 + down1_back))

time: 184 us -> 170 us (0.924)
  the two profiles are of different devices: /device:TPU:6 before, /device:TPU:96 now
where the time goes in v1:
time: 170 us; the launch traced here: 169 us
  blocking collectives  70 us (41%)
  Pallas kernels  32.7 us (19%)
  starting transfers between devices  32.3 us (19%)
  waiting for transfers between devices  18.3 us (11%)
  other arithmetic  8.6 us (5%)
  local copies, waits for them, and re-layouts  5.98 us (4%)
    all_to_all x2, blocking collectives, hand_out(): return lax.all_to_all(spread, axis, 0, 0, tiled=True)  49.9 us
    ppermute x11, starting transfers between devices, shift(): lax.ppermute(value, axis, [(source, source + steps) for source in range(f...  32.3 us
    all_to_all x1, blocking collectives, add_shares(): return lax.all_to_all(shares, axis, 0, 0, tiled=True).sum(axis=0)  20 us
    ppermute x11, waiting for transfers between devices, shift(): lax.ppermute(value, axis, [(source, source + steps) for source in range(f...  18.3 us
    pallas_call x1, Pallas kernels, second_call(): call(second_kernel, SLOTS // GROUP, [SCALARS] + [ANYWHERE] * 10 + [FIELDS...  16.5 us
    pallas_call x1, Pallas kernels, first_call(): call(first_kernel, SLOTS // GROUP, [SCALARS] + [ANYWHERE] * 5 + [FIELDS,...  9.91 us
    pallas_call x1, Pallas kernels, prepare_call(): call(prepare_kernel, SLOTS // PREPARED, [SCALARS, WHOLE, pl.BlockSpec((PR...  6.31 us
  transfers between devices with their start and end apart: 11, of which 3 were waited for; matrix products, arithmetic and copies ran while one was open for 4% of the time, Pallas kernels for 10%

profile of v1, /device:TPU:96, one launch (start us, length us, event | category | flops | bytes accessed | tf_op | source)
XLA Modules:
  0.0 169.5 jit_solution(12209153106540286376)
XLA Ops:
  0.6 0.0 copy-start
  0.6 2.8 %fusion = (f32[2,256,256]{2,1,0:T(8,128)}, f32[2,256,256]{2,1,0:T(8,128)S(1)}, f32[2,256,256]{2,1,0:T(8,128)S(1)}, f32[2,256,256]{2,1,0:T(8,128)}) fusion(f32[4,256,512]{2,1,0:T(8,128)} %own.3), kind=kLoop, calls=%fused_computation.5 | loop fusion | bytes 4194304 | tf_op jit(solution)/shard_map/slice | solution.py:500
  3.5 0.0 copy-start.4
  3.5 0.0 copy-start.5
  3.5 1.4 collective-permute-start.1
  4.9 0.0 copy-done
  4.9 0.1 slice.23
  5.0 1.9 %collective-permute-start = (f32[4,256,256]{2,1,0:T(8,128)S(1)}, f32[4,256,256]{2,1,0:T(8,128)}, u32[]{:S(2)}, u32[]{:S(2)}) collective-permute-start(f32[4,256,256]{2,1,0:T(8,128)S(1)} %slice.23), channel_id=1, source_target_pairs={{1,0},{2,1},{3,2},{4,3},{5,4},{6,5},{7,6},{9,8},{10,9},{11,10},{12... | collective-permute-start | bytes 3145736 | tf_op jit(solution)/shard_map/ppermute | solution.py:473
  6.9 1.3 collective-permute-start.3
  8.2 1.3 collective-permute-start.2
  10.2 0.0 copy-done.4
  10.2 0.2 copy.12
  10.4 0.2 copy.13
  10.6 10.0 %collective-permute-done.1.down0.down0_one = f32[2,256,256]{2,1,0:T(8,128)} collective-permute-done((f32[2,256,256]{2,1,0:T(8,128)}, f32[2,256,256]{2,1,0:T(8,128)}, u32[]{:S(2)}, u32[]{:S(2)}) %collective-permute-start.1) | collective-permute-done | bytes 524320 | tf_op jit(solution)/shard_map/ppermute | solution.py:473
  20.6 1.9 %collective-permute-start.4 = (f32[2,256,256]{2,1,0:T(8,128)}, f32[2,256,256]{2,1,0:T(8,128)S(1)}, u32[]{:S(2)}, u32[]{:S(2)}) collective-permute-start(f32[2,256,256]{2,1,0:T(8,128)} %collective-permute-done.1.down0.down0_one), channel_id=1, source_target_pairs={{1,0},{2,1},{3,2},{4,3},{5,4},{6,5},{7,6},{9,8},{10,9},{11,10},{12... | collective-permute-start | bytes 1572872 | tf_op jit(solution)/shard_map/ppermute | solution.py:473
  22.5 0.0 copy-done.5
  22.6 0.7 pad_add_fusion.meta
  23.2 1.0 pad_maximum_fusion.1.twice
  24.3 6.3 %shard_map.95 = (f32[8,256,256]{2,1,0:T(8,128)}, f32[8,2,256,256]{3,2,1,0:T(8,128)}) custom-call(s32[17]{0:T(128)} %pad_add_fusion.meta, f32[2,2,512,128]{3,2,1,0:T(8,128)} %pad_maximum_fusion.1.twice, f32[8,256,256]{2,1,0:T(8,128)} %amp.1, bf16[2,256,256]{2,1,0:T(8,128)(2,1)} %constant.23.clone.fold), custom_call_target="tpu_custom_call" | custom-call | flops 1610612736 | bytes 12582912 | tf_op jit(solution)/shard_map/pallas_call | solution.py:420
  30.6 1.3 collective-permute-start.5
  31.9 0.0 collective-permute-done.3.down1.down1_one
  31.9 0.0 collective-permute-done.right
  31.9 0.0 collective-permute-done.4.corner.corner_one
  31.9 0.0 copy-start.6
  31.9 0.8 copy-done.6
  32.7 9.9 %shard_map.96.prop = f32[8,2,256,256]{3,2,1,0:T(8,128)} custom-call(s32[17]{0:T(128)} %pad_add_fusion.meta, f32[4,256,512]{2,1,0:T(8,128)} %own.3, f32[4,256,256]{2,1,0:T(8,128)} %collective-permute-done.right, f32[2,256,256]{2,1,0:T(8,128)} %collective-permute-done.1.down0.down0_one, f32[2,256,256]{2,1,0:T(8,128)} %collective-permute-done.3.down1.down1_one, ...), custom_call_target="tpu_custom_call" | custom-call | flops 6442450944 | bytes 12582912 | tf_op jit(solution)/shard_map/pallas_call | solution.py:435
  42.6 0.5 collective-permute-done.2.down0_two
  43.1 2.2 %collective-permute-start.6 = (f32[2,256,256]{2,1,0:T(8,128)}, f32[2,256,256]{2,1,0:T(8,128)S(1)}, u32[]{:S(2)}, u32[]{:S(2)}) collective-permute-start(f32[2,256,256]{2,1,0:T(8,128)} %collective-permute-done.2.down0_two), channel_id=1, source_target_pairs={{1,0},{2,1},{3,2},{4,3},{5,4},{6,5},{7,6},{9,8},{10,9},{11,10},{12... | collective-permute-start | bytes 1572872 | tf_op jit(solution)/shard_map/ppermute | solution.py:473
  45.2 7.8 %collective-permute-done.5.down1_two = f32[2,256,256]{2,1,0:T(8,128)S(1)} collective-permute-done((f32[2,256,256]{2,1,0:T(8,128)S(1)}, f32[2,256,256]{2,1,0:T(8,128)S(1)}, u32[]{:S(2)}, u32[]{:S(2)}) %collective-permute-start.5) | collective-permute-done | bytes 524320 | tf_op jit(solution)/shard_map/ppermute | solution.py:473
  53.1 0.0 copy-start.7
  53.1 0.0 collective-permute-done.6.corner_two
  53.1 0.0 copy-start.8
  53.1 0.8 copy-done.7
  53.9 0.2 copy-done.8
  54.0 16.5 %shard_map.97 = (f32[4,256,256]{2,1,0:T(8,128)}, f32[4,256,256]{2,1,0:T(8,128)}, f32[4,256,256]{2,1,0:T(8,128)}, f32[4,256,256]{2,1,0:T(8,128)}, f32[4,256,256]{...) custom-call(s32[17]{0:T(128)} %pad_add_fusion.meta, f32[4,256,512]{2,1,0:T(8,128)} %own.3, ...), custom_call_target="tpu_custom_call" | custom-call | flops 12884901888 | bytes 12582912 | tf_op jit(solution)/shard_map/pallas_call | solution.py:451
  70.6 0.0 copy-start.3
  70.6 13.1 %collective-permute-start.9 = (f32[4,256,256]{2,1,0:T(8,128)}, f32[4,256,256]{2,1,0:T(8,128)}, u32[]{:S(2)}, u32[]{:S(2)}) collective-permute-start(f32[4,256,256]{2,1,0:T(8,128)} %get-tuple-element.37), channel_id=1, source_target_pairs={{0,1},{1,2},{2,3},{3,4},{4,5},{5,6},{6,7},{8,9},{9,10},{10,11},{11... | collective-permute-start | bytes 3145736 | tf_op jit(solution)/shard_map/ppermute | solution.py:473
  83.7 20.0 %all_to_all.15 = f32[16,32,256]{2,1,0:T(8,128)S(1)} all-to-all(f32[16,32,256]{2,1,0:T(8,128)} %bitcast.11), channel_id=1, replica_groups=mesh['row'=16,'col'=8] {'row'}, dimensions={0} | all-to-all | bytes 1048576 | tf_op jit(solution)/shard_map/all_to_all | solution.py:479
  103.8 1.9 %collective-permute-start.7 = (f32[4,256,256]{2,1,0:T(8,128)}, f32[4,256,256]{2,1,0:T(8,128)}, u32[]{:S(2)}, u32[]{:S(2)}) collective-permute-start(f32[4,256,256]{2,1,0:T(8,128)} %get-tuple-element.32), channel_id=1, source_target_pairs={{0,1},{1,2},{2,3},{3,4},{4,5},{5,6},{6,7},{8,9},{9,10},{10,11},{11... | collective-permute-start | bytes 3145736 | tf_op jit(solution)/shard_map/ppermute | solution.py:473
  105.7 2.5 %collective-permute-start.8 = (f32[4,256,256]{2,1,0:T(8,128)}, f32[4,256,256]{2,1,0:T(8,128)S(1)}, u32[]{:S(2)}, u32[]{:S(2)}) collective-permute-start(f32[4,256,256]{2,1,0:T(8,128)} %get-tuple-element.34), channel_id=1, source_target_pairs={{0,8},{8,16},{16,24},{24,32},{32,40},{40,48},{48,56},{56,64},{64,7... | collective-permute-start | bytes 3145736 | tf_op jit(solution)/shard_map/ppermute | solution.py:473
  108.2 0.0 collective-permute-done.9
  108.3 0.0 copy-done.3
  108.3 2.3 %add.14 = f32[4,256,256]{2,1,0:T(8,128)} add(f32[4,256,256]{2,1,0:T(8,128)S(1)} %copy-done.3, f32[4,256,256]{2,1,0:T(8,128)} %collective-permute-done.9) | non-fusion elementwise | flops 262144 | bytes 3145728 | tf_op jit(solution)/shard_map/add | solution.py:518
  110.6 0.0 copy-start.2
  110.6 3.5 %collective-permute-start.10 = (f32[4,256,256]{2,1,0:T(8,128)}, f32[4,256,256]{2,1,0:T(8,128)}, u32[]{:S(2)}, u32[]{:S(2)}) collective-permute-start(f32[4,256,256]{2,1,0:T(8,128)} %add.14), channel_id=1, source_target_pairs={{0,8},{8,16},{16,24},{24,32},{32,40},{40,48},{48,56},{56,64},{64,7... | collective-permute-start | bytes 3145736 | tf_op jit(solution)/shard_map/ppermute | solution.py:473
  114.1 10.4 %all_to_all.16 = f32[8,32,256]{2,1,0:T(8,128)S(1)} all-to-all(f32[8,32,256]{2,1,0:T(8,128)S(1)} %broadcast_in_dim.4), channel_id=1, replica_groups=mesh['row'=16,'col'=8] {'col'}, dimensions={0} | all-to-all | bytes 524288 | tf_op jit(solution)/shard_map/all_to_all | solution.py:484
  124.6 0.0 copy-start.1
  124.6 39.6 %all_to_all.17 = f32[16,32,256]{2,1,0:T(8,128)S(1)} all-to-all(f32[16,32,256]{2,1,0:T(8,128)S(1)} %broadcast_in_dim.5), channel_id=1, replica_groups=mesh['row'=16,'col'=8] {'row'}, dimensions={0} | all-to-all | bytes 1048576 | tf_op jit(solution)/shard_map/all_to_all | solution.py:484
  164.1 0.0 collective-permute-done.7
  164.1 0.0 copy-done.2
  164.1 1.4 add.12
  165.5 0.0 collective-permute-done.8
  165.5 0.0 copy-done.1
  165.5 0.1 add.13
  165.7 0.0 collective-permute-done.10
  165.7 1.4 add.15
  167.0 1.6 pad_maximum_fusion
  168.7 0.8 copy.16
  (5 shorter events, 0.1 us)
Async XLA Ops:
  0.6 4.3 %copy-start = (f32[4,256,512]{2,1,0:T(8,128)S(1)}, f32[4,256,512]{2,1,0:T(8,128)}, u32[]{:S(2)}) copy-start(f32[4,256,512]{2,1,0:T(8,128)} %own.3) | copy-start | bytes 6291460
  3.5 6.7 %copy-start.4 = (f32[2,256,256]{2,1,0:T(8,128)S(1)}, f32[2,256,256]{2,1,0:T(8,128)}, u32[]{:S(2)}) copy-start(f32[2,256,256]{2,1,0:T(8,128)} %param.9) | copy-start | bytes 1572868
  3.5 19.1 %copy-start.5 = (s32[8,2]{0,1:T(2,128)S(1)}, s32[8,2]{0,1:T(2,128)}, u32[]{:S(2)}) copy-start(s32[8,2]{0,1:T(2,128)} %param.10) | copy-start | bytes 196
  3.5 17.1 %collective-permute-start.1 = (f32[2,256,256]{2,1,0:T(8,128)}, f32[2,256,256]{2,1,0:T(8,128)}, u32[]{:S(2)}, u32[]{:S(2)}) collective-permute-start(f32[2,256,256]{2,1,0:T(8,128)} %get-tuple-element.43), channel_id=1, source_target_pairs={{8,0},{16,8},{24,16},{32,24},{40,32},{48,40},{56,48},{64,56},{72,6... | collective-permute-start | bytes 1572872 | tf_op jit(solution)/shard_map/ppermute | solution.py:473
  5.0 26.9 %collective-permute-start = (f32[4,256,256]{2,1,0:T(8,128)S(1)}, f32[4,256,256]{2,1,0:T(8,128)}, u32[]{:S(2)}, u32[]{:S(2)}) collective-permute-start(f32[4,256,256]{2,1,0:T(8,128)S(1)} %slice.23), channel_id=1, source_target_pairs={{1,0},{2,1},{3,2},{4,3},{5,4},{6,5},{7,6},{9,8},{10,9},{11,10},{12... | collective-permute-start | bytes 3145736 | tf_op jit(solution)/shard_map/ppermute | solution.py:473
  6.9 24.9 %collective-permute-start.3 = (f32[2,256,256]{2,1,0:T(8,128)}, f32[2,256,256]{2,1,0:T(8,128)}, u32[]{:S(2)}, u32[]{:S(2)}) collective-permute-start(f32[2,256,256]{2,1,0:T(8,128)} %get-tuple-element.40), channel_id=1, source_target_pairs={{8,0},{16,8},{24,16},{32,24},{40,32},{48,40},{56,48},{64,56},{72,6... | collective-permute-start | bytes 1572872 | tf_op jit(solution)/shard_map/ppermute | solution.py:473
  8.2 34.8 %collective-permute-start.2 = (f32[2,256,256]{2,1,0:T(8,128)S(1)}, f32[2,256,256]{2,1,0:T(8,128)}, u32[]{:S(2)}, u32[]{:S(2)}) collective-permute-start(f32[2,256,256]{2,1,0:T(8,128)S(1)} %get-tuple-element.41), channel_id=1, source_target_pairs={{8,0},{16,8},{24,16},{32,24},{40,32},{48,40},{56,48},{64,56},{72,6... | collective-permute-start | bytes 1572872 | tf_op jit(solution)/shard_map/ppermute | solution.py:473
  20.6 11.3 %collective-permute-start.4 = (f32[2,256,256]{2,1,0:T(8,128)}, f32[2,256,256]{2,1,0:T(8,128)S(1)}, u32[]{:S(2)}, u32[]{:S(2)}) collective-permute-start(f32[2,256,256]{2,1,0:T(8,128)} %collective-permute-done.1.down0.down0_one), channel_id=1, source_target_pairs={{1,0},{2,1},{3,2},{4,3},{5,4},{6,5},{7,6},{9,8},{10,9},{11,10},{12... | collective-permute-start | bytes 1572872 | tf_op jit(solution)/shard_map/ppermute | solution.py:473
  30.6 22.5 %collective-permute-start.5 = (f32[2,256,256]{2,1,0:T(8,128)S(1)}, f32[2,256,256]{2,1,0:T(8,128)S(1)}, u32[]{:S(2)}, u32[]{:S(2)}) collective-permute-start(f32[2,256,256]{2,1,0:T(8,128)S(1)} %get-tuple-element.24), channel_id=1, source_target_pairs={{8,0},{16,8},{24,16},{32,24},{40,32},{48,40},{56,48},{64,56},{72,6... | collective-permute-start | bytes 1572872 | tf_op jit(solution)/shard_map/ppermute | solution.py:473
  31.9 0.8 copy-start.6
  43.1 10.0 %collective-permute-start.6 = (f32[2,256,256]{2,1,0:T(8,128)}, f32[2,256,256]{2,1,0:T(8,128)S(1)}, u32[]{:S(2)}, u32[]{:S(2)}) collective-permute-start(f32[2,256,256]{2,1,0:T(8,128)} %collective-permute-done.2.down0_two), channel_id=1, source_target_pairs={{1,0},{2,1},{3,2},{4,3},{5,4},{6,5},{7,6},{9,8},{10,9},{11,10},{12... | collective-permute-start | bytes 1572872 | tf_op jit(solution)/shard_map/ppermute | solution.py:473
  53.1 0.8 copy-start.7
  53.1 1.0 copy-start.8
  70.6 37.7 %copy-start.3 = (f32[4,256,256]{2,1,0:T(8,128)S(1)}, f32[4,256,256]{2,1,0:T(8,128)}, u32[]{:S(2)}) copy-start(f32[4,256,256]{2,1,0:T(8,128)} %get-tuple-element.36) | copy-start | bytes 3145732
  70.6 37.7 %collective-permute-start.9 = (f32[4,256,256]{2,1,0:T(8,128)}, f32[4,256,256]{2,1,0:T(8,128)}, u32[]{:S(2)}, u32[]{:S(2)}) collective-permute-start(f32[4,256,256]{2,1,0:T(8,128)} %get-tuple-element.37), channel_id=1, source_target_pairs={{0,1},{1,2},{2,3},{3,4},{4,5},{5,6},{6,7},{8,9},{9,10},{10,11},{11... | collective-permute-start | bytes 3145736 | tf_op jit(solution)/shard_map/ppermute | solution.py:473
  103.8 60.3 %collective-permute-start.7 = (f32[4,256,256]{2,1,0:T(8,128)}, f32[4,256,256]{2,1,0:T(8,128)}, u32[]{:S(2)}, u32[]{:S(2)}) collective-permute-start(f32[4,256,256]{2,1,0:T(8,128)} %get-tuple-element.32), channel_id=1, source_target_pairs={{0,1},{1,2},{2,3},{3,4},{4,5},{5,6},{6,7},{8,9},{9,10},{10,11},{11... | collective-permute-start | bytes 3145736 | tf_op jit(solution)/shard_map/ppermute | solution.py:473
  105.7 59.8 %collective-permute-start.8 = (f32[4,256,256]{2,1,0:T(8,128)}, f32[4,256,256]{2,1,0:T(8,128)S(1)}, u32[]{:S(2)}, u32[]{:S(2)}) collective-permute-start(f32[4,256,256]{2,1,0:T(8,128)} %get-tuple-element.34), channel_id=1, source_target_pairs={{0,8},{8,16},{16,24},{24,32},{32,40},{40,48},{48,56},{56,64},{64,7... | collective-permute-start | bytes 3145736 | tf_op jit(solution)/shard_map/ppermute | solution.py:473
  110.6 53.5 %copy-start.2 = (f32[4,256,256]{2,1,0:T(8,128)S(1)}, f32[4,256,256]{2,1,0:T(8,128)}, u32[]{:S(2)}) copy-start(f32[4,256,256]{2,1,0:T(8,128)} %get-tuple-element.27) | copy-start | bytes 3145732
  110.6 55.1 %collective-permute-start.10 = (f32[4,256,256]{2,1,0:T(8,128)}, f32[4,256,256]{2,1,0:T(8,128)}, u32[]{:S(2)}, u32[]{:S(2)}) collective-permute-start(f32[4,256,256]{2,1,0:T(8,128)} %add.14), channel_id=1, source_target_pairs={{0,8},{8,16},{16,24},{24,32},{32,40},{40,48},{48,56},{56,64},{64,7... | collective-permute-start | bytes 3145736 | tf_op jit(solution)/shard_map/ppermute | solution.py:473
  124.6 40.9 %copy-start.1 = (f32[4,256,256]{2,1,0:T(8,128)S(1)}, f32[4,256,256]{2,1,0:T(8,128)}, u32[]{:S(2)}) copy-start(f32[4,256,256]{2,1,0:T(8,128)} %get-tuple-element.33) | copy-start | bytes 3145732

commit v2 on v0

--- a/solution.py
+++ b/solution.py
@@ -192,7 +192,7 @@
             )
         return carry
 
-    lax.fori_loop(0, W // CHUNK, load, 0, unroll=2)
+    lax.fori_loop(0, W // CHUNK, load, 0, unroll=True)
     at = pl.multiple_of(border * CHUNK, CHUNK)
     here = pl.ds(at, CHUNK)
     in_top, in_first = masks(row, col, at)
@@ -205,25 +205,26 @@
     row, col, first, second = geometry(meta, slot)
     border = row // CHUNK
     zero = jnp.zeros((CHUNK, W), F32)
+    alive = slot < meta[0]
 
     def add(i, carry):
         at = pl.multiple_of(i * CHUNK, CHUNK)
         here = pl.ds(at, CHUNK)
         in_top, in_first = masks(row, col, at)
         low = (i < border).astype(jnp.int32)
-        keep = jnp.logical_or(in_top, i < border)
+        keep = jnp.logical_and(jnp.logical_or(in_top, i < border), alive)
         for p in planes:
             value = jnp.where(keep, win[u, p, here, :], zero)
             gext[low, p, here, pl.ds(first, W)] += jnp.where(in_first, value, zero)
             gext[low, p, here, pl.ds(second, W)] += jnp.where(in_first, zero, value)
         return carry
 
-    lax.fori_loop(0, W // CHUNK, add, 0, unroll=2)
+    lax.fori_loop(0, W // CHUNK, add, 0, unroll=True)
     at = pl.multiple_of(border * CHUNK, CHUNK)
     here = pl.ds(at, CHUNK)
     in_top, in_first = masks(row, col, at)
     for p in planes:
-        value = jnp.where(in_top, zero, win[u, p, here, :])
+        value = jnp.where(jnp.logical_and(jnp.logical_not(in_top), alive), win[u, p, here, :], zero)
         gext[1, p, here, pl.ds(first, W)] += jnp.where(in_first, value, zero)
         gext[1, p, here, pl.ds(second, W)] += jnp.where(in_first, zero, value)
 
@@ -239,7 +240,7 @@
     row, col, _, _ = geometry(meta, slot)
     for p in range(2):
         here = pl.ds(W - row, W)
-        value = pltpu.roll(part[u, p], W - col, 1)
+        value = jnp.where(slot < meta[0], pltpu.roll(part[u, p], W - col, 1), 0.0)
         acc[p, 0, here, :] += value[:, :HALF_W]
         acc[p, 1, here, :] += value[:, HALF_W:]
 
@@ -267,7 +268,7 @@
         copy.wait()
 
 
-def prepare_kernel(meta, twice, amp, fold, amp_out, turned):
+def prepare_kernel(meta, probe, amp, fold, amp_out, turned, twice):
     step = pl.program_id(0)
 
     def fold_amplitudes(u):
@@ -279,6 +280,14 @@
         out = dot(fold[1], lanes(*(right_way[i * W : (i + 1) * W].astype(BF16) for i in range(3))))
         amp_out[u] = out[:, :W] + out[:, W : 2 * W] + out[:, 2 * W :]
 
+    @pl.when(step == 0)
+    def double_probe():
+        for p in range(2):
+            for half in range(2):
+                part = probe[p, :, half * HALF_W : (half + 1) * HALF_W]
+                twice[p, half, :W, :] = part
+                twice[p, half, W:, :] = part
+
     for u in range(PREPARED):
         fold_amplitudes(u)
         turn_probe(meta, step * PREPARED + u, twice, turned, u)
@@ -289,7 +298,8 @@
 
     @pl.when(step == 0)
     def begin():
-        refs = (own.at[pl.ds(0, 2)], right.at[pl.ds(0, 2)], down0, down1, corner)
+        one = pl.ds(0, 2)
+        refs = (own.at[one], right.at[one], down0, down1, corner)
         wait_copies(start_copies(tile_copies(refs, ext, sems)))
 
     @pl.when(step * GROUP < meta[0])
@@ -303,8 +313,8 @@
             put(f, prop, u)
 
 
-def second_kernel(meta, own, right, down0_one, down0_two, down1_one, down1_two, corner_one, corner_two, turned_in, hop_in,
-                  prop, amp, dft, gown0, gown1, gright, gdown0, gdown1, gcorner, gprobe,
+def second_kernel(meta, own, right, down0_one, down0_two, down1_one, corner_one, turned_in, hop_in, down1_two, corner_two,
+                  prop, amp, dft, gown, gright, gdown0, gdown1, gcorner, gprobe,
                   ext, gext, acc, turned, hop, win, sems):
     step = pl.program_id(0)
     group = range(GROUP)
@@ -367,7 +377,7 @@
 
         for u in group:
             slot = step * GROUP + u
-            pl.when(slot < meta[0])(lambda: finish(slot, u))
+            finish(slot, u)
 
     @pl.when(step == SLOTS // GROUP - 1)
     def end():
@@ -377,8 +387,7 @@
             (gext.at[1, :, :, pl.ds(TC, W)], gcorner, sem.at[1]),
             (gext.at[1, :, :, pl.ds(0, W)], gdown0, sem.at[2]),
             (gext.at[0, :, :, pl.ds(TC, W)], gright, sem.at[3]),
-            (gext.at[0, :, :, pl.ds(0, W)], gown0, sem.at[4]),
-            (gext.at[0, :, :, pl.ds(W, W)], gown1, sems.at[1, 0]),
+            (gext.at[0, :, :, pl.ds(0, TC)], gown, sem.at[4]),
         ])
         for p in range(2):
             gprobe[p] = lanes(acc[p, 0, :W, :] + acc[p, 0, W:, :], acc[p, 1, :W, :] + acc[p, 1, W:, :])
@@ -399,7 +408,7 @@
 FIELDS_SHAPE = shape(SLOTS, 2, W, W)
 
 
-def call(kernel, steps, in_specs, out_specs, out_shape, scratch, products):
+def call(kernel, steps, in_specs, out_specs, out_shape, scratch, products, mebibytes):
     return pl.pallas_call(
         kernel,
         grid=(steps,),
@@ -408,10 +417,10 @@
         out_shape=out_shape,
         scratch_shapes=scratch,
         compiler_params=pltpu.CompilerParams(
-            vmem_limit_bytes=56 * 2**20, dimension_semantics=("arbitrary",)
+            vmem_limit_bytes=mebibytes * 2**20, dimension_semantics=("arbitrary",)
         ),
         cost_estimate=pl.CostEstimate(
-            flops=SLOTS * products * 2 * W**3, bytes_accessed=12 * 2**20, transcendentals=0
+            flops=SLOTS * products * 2 * W**3, bytes_accessed=products * 2**18, transcendentals=0
         ),
     )
 
@@ -426,8 +435,9 @@
             pl.BlockSpec((PREPARED, 2, W, W), lambda i: (i, 0, 0, 0)),
         ],
         [shape(SLOTS, W, W), FIELDS_SHAPE],
-        [],
-        6,
+        [pltpu.VMEM((2, 2, 2 * W, HALF_W), F32)],
+        0,
+        16,
     )(*args)
 
 
@@ -435,7 +445,7 @@
     return call(
         first_kernel,
         SLOTS // GROUP,
-        [SCALARS] + [ANYWHERE] * 5 + [FIELDS, WHOLE],
+        [SCALARS] + [ANYWHERE] * 3 + [WHOLE, WHOLE, FIELDS, WHOLE],
         FIELDS,
         FIELDS_SHAPE,
         [
@@ -444,6 +454,7 @@
             pltpu.SemaphoreType.DMA((5,)),
         ],
         24,
+        32,
     )(*args)
 
 
@@ -451,9 +462,9 @@
     return call(
         second_kernel,
         SLOTS // GROUP,
-        [SCALARS] + [ANYWHERE] * 10 + [FIELDS, PLANES, WHOLE],
-        [ANYWHERE] * 6 + [WHOLE],
-        [shape(4, W, W)] * 6 + [shape(2, W, W)],
+        [SCALARS] + [ANYWHERE] * 8 + [WHOLE, WHOLE, FIELDS, PLANES, WHOLE],
+        [ANYWHERE] * 5 + [WHOLE],
+        [shape(4, W, TC)] + [shape(4, W, W)] * 4 + [shape(2, W, W)],
         [
             pltpu.VMEM((2, 4, W, EXT), F32),
             pltpu.VMEM((2, 4, W, EXT), F32),
@@ -464,7 +475,30 @@
             pltpu.SemaphoreType.DMA((3, 5)),
         ],
         48,
+        50,
     )(*args)
+
+
+def add_kernel(base, *refs):
+    parts, out = refs[:-1], refs[-1]
+    for i, part in enumerate(parts):
+        here = pl.ds(i * W, W)
+        out[:, :, here] = base[:, :, here] + part[...]
+
+
+def add_call(base, *parts):
+    block = pl.BlockSpec((1, W, W * len(parts)), lambda i: (i, 0, 0))
+    part = pl.BlockSpec((1, W, W), lambda i: (i, 0, 0))
+    return pl.pallas_call(
+        add_kernel,
+        grid=(4,),
+        in_specs=[block] + [part] * len(parts),
+        out_specs=block,
+        out_shape=shape(4, W, TC),
+        input_output_aliases={0: 0},
+        compiler_params=pltpu.CompilerParams(vmem_limit_bytes=8 * 2**20),
+        cost_estimate=pl.CostEstimate(flops=2**19, bytes_accessed=2**22, transcendentals=0),
+    )(base, *parts)
 
 
 def shift(value, axis, steps):
@@ -484,9 +518,11 @@
     return lax.all_to_all(spread, axis, 0, 0, tiled=True)
 
 
-def probe_twice(probe):
-    halves = probe.reshape(2, W, 2, HALF_W).transpose(0, 2, 1, 3)
-    return jnp.concatenate([halves, halves], axis=2)
+def ring_sum(value, pairs):
+    first = lax.ppermute(value, "row", pairs)
+    second = lax.ppermute(first, "row", pairs)
+    third = lax.ppermute(second, "row", pairs)
+    return (value + second) + (first + third)
 
 
 def body(object_slab, probe_wave, scan_offsets, live_counts, amplitudes):
@@ -495,33 +531,34 @@
     local_cols = scan_offsets[:, 1] - lax.axis_index("col") * cols_tile
     meta = jnp.concatenate([live_counts, local_rows, local_cols])
     hop, dft, fold = jnp.asarray(hop_tables()), jnp.asarray(dft_tables()), jnp.asarray(fold_tables())
-    twice = probe_twice(probe_wave)
     down0_one = shift(object_slab[:2, :, :W], "row", -1)
     down1_one = shift(object_slab[:2, :, W:], "row", -1)
     right = shift(object_slab[:, :, :W], "col", -1)
     down0_two = shift(object_slab[2:, :, :W], "row", -1)
-    down0_one, last_part = lax.optimization_barrier((down0_one, object_slab[2:, :, W:]))
+    amp, turned = prepare_call(meta, probe_wave, amplitudes, fold)
+    down0_one, turned, last_part = lax.optimization_barrier((down0_one, turned, object_slab[2:, :, W:]))
+    corner_one = shift(down0_one, "col", -1)
     down1_two = shift(last_part, "row", -1)
-    corner_one = shift(down0_one, "col", -1)
-    amp, turned = prepare_call(meta, twice, amplitudes, fold)
     prop = first_call(meta, object_slab, right, down0_one, down1_one, corner_one, turned, hop)
     down0_two, prop = lax.optimization_barrier((down0_two, prop))
     corner_two = shift(down0_two, "col", -1)
-    gown0, gown1, gright, gdown0, gdown1, gcorner, gprobe = second_call(
-        meta, object_slab, right, down0_one, down0_two, down1_one, down1_two, corner_one, corner_two, turned, hop,
+    gown, gright, gdown0, gdown1, gcorner, gprobe = second_call(
+        meta, object_slab, right, down0_one, down0_two, down1_one, corner_one, turned, hop, down1_two, corner_two,
         prop, amp, dft,
     )
+    side = lax.axis_size("row") // 4
+    to_left_x = [(i, (i - side) % (4 * side)) for i in range(4 * side)]
+    to_left_y = [(i, i - i % side + (i - 1) % side) for i in range(4 * side)]
     corner_back = shift(gcorner, "col", 1)
     down1_back = shift(gdown1, "row", 1)
-    share = add_shares(gprobe, "row")
-    gdown0, gright, share = lax.optimization_barrier((gdown0 + corner_back, gright, share))
+    share = add_shares(gprobe, "col")
+    gdown0, share = lax.optimization_barrier((gdown0 + corner_back, share))
     down0_back = shift(gdown0, "row", 1)
     right_back = shift(gright, "col", 1)
-    share = hand_out(share, "col").sum(axis=0)
-    own0, own1 = lax.optimization_barrier((gown0 + right_back, gown1 + down1_back))
-    probe_grad = hand_out(share, "row").reshape(probe_wave.shape)
-    object_grad = jnp.concatenate([own0 + down0_back, own1], axis=2)
-    return object_grad, probe_grad
+    share = ring_sum(ring_sum(share, to_left_x), to_left_y)
+    gown, share = lax.optimization_barrier((add_call(gown, right_back, down1_back), share))
+    probe_grad = hand_out(share, "col").reshape(probe_wave.shape)
+    return add_call(gown, down0_back), probe_grad
 
 
 def solution(mesh):

time: 184 us -> 157 us (0.85); the launches traced: 181 us -> 156 us
  starting transfers between devices: 77.2 us -> 55.8 us
  waiting for transfers between devices: 22.4 us -> 41.5 us
  Pallas kernels: 48.2 us -> 34 us
  other arithmetic: 10.1 us -> 1.83 us
    all_to_all x1 -> x0, starting transfers between devices: 37.5 us -> none  [hand_out(): return lax.all_to_all(spread, axis, 0, 0, tiled=True)]
    ppermute x0 -> x6, waiting for transfers between devices: none -> 17.9 us  [the longest x2 7.77 us: ring_sum(): second = lax.ppermute(first, 'row', pairs)]
    pallas_call x2 -> x4, Pallas kernels: 41.9 us -> 30.3 us  [the longest x1 16.7 us: second_call(): call(second_kernel, SLOTS // GROUP, [SCALARS] + [ANYWHERE] * 8 + [WHOLE,...]
    ppermute x0 -> x6, starting transfers between devices: none -> 8.7 us  [the longest x2 3.57 us: ring_sum(): third = lax.ppermute(second, 'row', pairs)]
    all_to_all x1 -> x0, waiting for transfers between devices: 7.99 us -> none  [hand_out(): return lax.all_to_all(spread, axis, 0, 0, tiled=True)]
    all_to_all x1, starting transfers between devices: 7.33 us -> 14.6 us  [add_shares(): return lax.all_to_all(shares, axis, 0, 0, tiled=True).sum(axis=0)]
    ppermute x11, waiting for transfers between devices: 7.65 us -> 14.5 us  [shift(): lax.ppermute(value, axis, [(source, source + steps) for source in range(f...]
    add x4 -> x3, other arithmetic: 6.76 us -> 1.71 us  [the longest x1 1.68 us: body(): gdown0, share = lax.optimization_barrier((gdown0 + corner_back, share))]
  transfers between devices with their start and end apart: 13 -> 18, of which waited for: 5 -> 10; matrix products, arithmetic and copies ran while one was open for 5% -> 2% of each run, Pallas kernels for 11% -> 9%
where the time goes in v2:
time: 157 us; the launch traced here: 156 us
  starting transfers between devices  55.8 us (36%)
  waiting for transfers between devices  41.5 us (26%)
  Pallas kernels  34 us (22%)
  blocking collectives  13.2 us (8%)
  local copies, waits for them, and re-layouts  8.58 us (5%)
  other arithmetic  1.83 us (1%)
    ppermute x11, starting transfers between devices, shift(): lax.ppermute(value, axis, [(source, source + steps) for source in range(f...  32.5 us
    pallas_call x1, Pallas kernels, second_call(): call(second_kernel, SLOTS // GROUP, [SCALARS] + [ANYWHERE] * 8 + [WHOLE,...  16.7 us
    all_to_all x1, starting transfers between devices, add_shares(): return lax.all_to_all(shares, axis, 0, 0, tiled=True).sum(axis=0)  14.6 us
    ppermute x11, waiting for transfers between devices, shift(): lax.ppermute(value, axis, [(source, source + steps) for source in range(f...  14.5 us
    all_to_all x1, blocking collectives, hand_out(): return lax.all_to_all(spread, axis, 0, 0, tiled=True)  13.2 us
    all_to_all x1, waiting for transfers between devices, add_shares(): return lax.all_to_all(shares, axis, 0, 0, tiled=True).sum(axis=0)  9.08 us
    ppermute x2, waiting for transfers between devices, ring_sum(): second = lax.ppermute(first, 'row', pairs)  7.77 us
    ppermute x2, waiting for transfers between devices, ring_sum(): first = lax.ppermute(value, 'row', pairs)  7.6 us
  transfers between devices with their start and end apart: 18, of which 10 were waited for; matrix products, arithmetic and copies ran while one was open for 2% of the time, Pallas kernels for 9%

profile of v2, /device:TPU:6, one launch (start us, length us, event | category | flops | bytes accessed | tf_op | source)
XLA Modules:
  0.0 156.3 jit_solution(2283946192030202894)
XLA Ops:
  0.6 0.0 copy-start
  0.6 3.0 %fusion = (f32[2,256,256]{2,1,0:T(8,128)}, f32[2,256,256]{2,1,0:T(8,128)}, f32[2,256,256]{2,1,0:T(8,128)}, f32[2,256,256]{2,1,0:T(8,128)}) fusion(f32[4,256,512]{2,1,0:T(8,128)} %own.3), kind=kLoop, calls=%fused_computation.5 | loop fusion | bytes 4194304 | tf_op jit(solution)/shard_map/slice | solution.py:535
  3.7 0.0 copy-start.10
  3.7 0.0 copy-start.3
  3.7 5.3 %collective-permute-start.1 = (f32[2,256,256]{2,1,0:T(8,128)}, f32[2,256,256]{2,1,0:T(8,128)S(1)}, u32[]{:S(2)}, u32[]{:S(2)}) collective-permute-start(f32[2,256,256]{2,1,0:T(8,128)} %get-tuple-element.39), channel_id=1, source_target_pairs={{8,0},{16,8},{24,16},{32,24},{40,32},{48,40},{56,48},{64,56},{72,6... | collective-permute-start | bytes 1572872 | tf_op jit(solution)/shard_map/ppermute | solution.py:507
  9.0 0.0 copy-done
  9.0 1.1 slice.23
  10.1 1.3 collective-permute-start
  11.4 2.7 %collective-permute-start.3 = (f32[2,256,256]{2,1,0:T(8,128)}, f32[2,256,256]{2,1,0:T(8,128)}, u32[]{:S(2)}, u32[]{:S(2)}) collective-permute-start(f32[2,256,256]{2,1,0:T(8,128)} %get-tuple-element.36), channel_id=1, source_target_pairs={{8,0},{16,8},{24,16},{32,24},{40,32},{48,40},{56,48},{64,56},{72,6... | collective-permute-start | bytes 1572872 | tf_op jit(solution)/shard_map/ppermute | solution.py:507
  14.7 0.0 copy-done.10
  14.7 0.1 pad_add_fusion.meta
  14.8 0.0 copy-done.2
  14.8 0.0 copy-done.3
  14.8 1.6 %copy-done.1 = f32[8,256,256]{2,1,0:T(8,128)S(1)} copy-done((f32[8,256,256]{2,1,0:T(8,128)S(1)}, f32[8,256,256]{2,1,0:T(8,128)}, u32[]{:S(2)}) %copy-start.1) | copy-done | bytes 2097176
  16.4 3.7 %shard_map.95 = (f32[8,256,256]{2,1,0:T(8,128)S(1)}, f32[8,2,256,256]{3,2,1,0:T(8,128)S(1)}) custom-call(s32[17]{0:T(128)S(1)} %pad_add_fusion.meta, f32[2,256,256]{2,1,0:T(8,128)S(1)} %copy-done.2, f32[8,256,256]{2,1,0:T(8,128)S(1)} %copy-done.1, bf16[2,256,256]{2,1,0:T(8,128)(2,1)S(1)} %copy-done.3), custom_call_target="tpu_custom_call" | custom-call | tf_op jit(solution)/shard_map/pallas_call | solution.py:429
  20.1 0.0 copy-start.4
  20.1 0.0 copy-start.5
  20.1 1.5 collective-permute-done.1.down0.down0_one
  21.6 1.3 collective-permute-start.4
  22.9 0.0 copy-done.9
  22.9 6.4 %collective-permute-start.2 = (f32[2,256,256]{2,1,0:T(8,128)S(1)}, f32[2,256,256]{2,1,0:T(8,128)S(1)}, u32[]{:S(2)}, u32[]{:S(2)}) collective-permute-start(f32[2,256,256]{2,1,0:T(8,128)S(1)} %copy-done.9), channel_id=1, source_target_pairs={{8,0},{16,8},{24,16},{32,24},{40,32},{48,40},{56,48},{64,56},{72,6... | collective-permute-start | bytes 1572872 | tf_op jit(solution)/shard_map/ppermute | solution.py:507
  29.3 0.0 copy-done.8
  29.4 1.9 %collective-permute-start.5 = (f32[2,256,256]{2,1,0:T(8,128)S(1)}, f32[2,256,256]{2,1,0:T(8,128)S(1)}, u32[]{:S(2)}, u32[]{:S(2)}) collective-permute-start(f32[2,256,256]{2,1,0:T(8,128)S(1)} %copy-done.8), channel_id=1, source_target_pairs={{8,0},{16,8},{24,16},{32,24},{40,32},{48,40},{56,48},{64,56},{72,6... | collective-permute-start | bytes 1572872 | tf_op jit(solution)/shard_map/ppermute | solution.py:507
  31.3 1.4 collective-permute-done.3.down1.down1_one
  32.7 0.0 collective-permute-done.right
  32.7 0.0 collective-permute-done.4.corner.corner_one
  32.7 0.0 copy-done.6
  32.7 6.4 %shard_map.96.prop = f32[8,2,256,256]{3,2,1,0:T(8,128)S(1)} custom-call(s32[17]{0:T(128)S(1)} %pad_add_fusion.meta, f32[4,256,512]{2,1,0:T(8,128)S(1)} %copy-done, f32[4,256,256]{2,1,0:T(8,128)} %collective-permute-done.right, f32[2,256,256]{2,1,0:T(8,128)S(1)} %collective-permute-done.1.down0.down0_one, ...), custom_call_target="tpu_custom_call" | custom-call | flops 6442450944 | bytes 6291456 | tf_op jit(solution)/shard_map/pallas_call | solution.py:445
  39.1 0.0 copy-done.4
  39.1 0.0 copy-done.5
  39.1 0.0 copy-start.7
  39.1 2.0 %copy-done.7 = f32[8,2,256,256]{3,2,1,0:T(8,128)} copy-done((f32[8,2,256,256]{3,2,1,0:T(8,128)}, f32[8,2,256,256]{3,2,1,0:T(8,128)S(1)}, u32[]{:S(2)}) %copy-start.7) | copy-done | bytes 4194328
  41.2 2.7 %collective-permute-done.2.down0_two = f32[2,256,256]{2,1,0:T(8,128)S(1)} collective-permute-done((f32[2,256,256]{2,1,0:T(8,128)S(1)}, f32[2,256,256]{2,1,0:T(8,128)S(1)}, u32[]{:S(2)}, u32[]{:S(2)}) %collective-permute-start.2) | collective-permute-done | bytes 524320 | tf_op jit(solution)/shard_map/ppermute | solution.py:507
  43.9 1.5 collective-permute-start.6
  45.3 8.8 %collective-permute-done.5.down1_two = f32[2,256,256]{2,1,0:T(8,128)S(1)} collective-permute-done((f32[2,256,256]{2,1,0:T(8,128)S(1)}, f32[2,256,256]{2,1,0:T(8,128)S(1)}, u32[]{:S(2)}, u32[]{:S(2)}) %collective-permute-start.5) | collective-permute-done | bytes 524320 | tf_op jit(solution)/shard_map/ppermute | solution.py:507
  54.1 0.0 collective-permute-done.6.corner_two
  54.1 16.7 %shard_map.97 = (f32[4,256,512]{2,1,0:T(8,128)}, f32[4,256,256]{2,1,0:T(8,128)}, f32[4,256,256]{2,1,0:T(8,128)}, f32[4,256,256]{2,1,0:T(8,128)}, f32[4,256,256]{2,1,0:T(8,128)}, /*index=5*/f32[2,256,256]{2,1,0:T(8,128)}) custom-call(s32[17]{0:T(128)S(1)} %pad_add_fusion.meta, f32[4,256,512]{2,1,0:T(8,128)} %own.3, ...), custom_call_target="tpu_custom_call" | custom-call | flops 12884901888 | bytes 12582912 | tf_op jit(solution)/shard_map/pallas_call | solution.py:462
  70.9 3.5 %collective-permute-start.9 = (f32[4,256,256]{2,1,0:T(8,128)}, f32[4,256,256]{2,1,0:T(8,128)}, u32[]{:S(2)}, u32[]{:S(2)}) collective-permute-start(f32[4,256,256]{2,1,0:T(8,128)} %get-tuple-element.30), channel_id=1, source_target_pairs={{0,1},{1,2},{2,3},{3,4},{4,5},{5,6},{6,7},{8,9},{9,10},{10,11},{11... | collective-permute-start | bytes 3145736 | tf_op jit(solution)/shard_map/ppermute | solution.py:507
  74.3 14.6 %all-to-all-start = ((f32[8,64,256]{2,1,0:T(8,128)}), f32[8,64,256]{2,1,0:T(8,128)S(1)}, u32[]{:S(2)}, u32[]{:S(2)}) async-start(f32[8,64,256]{2,1,0:T(8,128)} %bitcast.2), calls=%async_computation | async-start | bytes 1048576 | tf_op jit(solution)/shard_map/all_to_all | solution.py:513
  88.9 2.5 %collective-permute-start.7 = (f32[4,256,256]{2,1,0:T(8,128)}, f32[4,256,256]{2,1,0:T(8,128)S(1)}, u32[]{:S(2)}, u32[]{:S(2)}) collective-permute-start(f32[4,256,256]{2,1,0:T(8,128)} %get-tuple-element.27), channel_id=1, source_target_pairs={{0,1},{1,2},{2,3},{3,4},{4,5},{5,6},{6,7},{8,9},{9,10},{10,11},{11... | collective-permute-start | bytes 3145736 | tf_op jit(solution)/shard_map/ppermute | solution.py:507
  91.4 3.2 %collective-permute-start.8 = (f32[4,256,256]{2,1,0:T(8,128)}, f32[4,256,256]{2,1,0:T(8,128)S(1)}, u32[]{:S(2)}, u32[]{:S(2)}) collective-permute-start(f32[4,256,256]{2,1,0:T(8,128)} %get-tuple-element.28), channel_id=1, source_target_pairs={{0,8},{8,16},{16,24},{24,32},{32,40},{40,48},{48,56},{56,64},{64,7... | collective-permute-start | bytes 3145736 | tf_op jit(solution)/shard_map/ppermute | solution.py:507
  94.6 9.1 %all-to-all-done = f32[8,64,256]{2,1,0:T(8,128)S(1)} async-done(((f32[8,64,256]{2,1,0:T(8,128)}), f32[8,64,256]{2,1,0:T(8,128)S(1)}, u32[]{:S(2)}, u32[]{:S(2)}) %all-to-all-start) | async-done | bytes 524320 | tf_op jit(solution)/shard_map/all_to_all | solution.py:513
  103.7 0.0 collective-permute-done.9
  103.7 1.7 %add.21 = f32[4,256,256]{2,1,0:T(8,128)S(1)} add(f32[4,256,256]{2,1,0:T(8,128)} %get-tuple-element.29, f32[4,256,256]{2,1,0:T(8,128)} %collective-permute-done.9) | non-fusion elementwise | flops 262144 | bytes 3145728 | tf_op jit(solution)/shard_map/add | solution.py:555
  105.4 0.6 collective-permute-start.10
  106.0 5.0 %collective-permute-done.10 = f32[64,256]{1,0:T(8,128)S(1)} collective-permute-done((f32[64,256]{1,0:T(8,128)S(1)}, f32[64,256]{1,0:T(8,128)S(1)}, u32[]{:S(2)}, u32[]{:S(2)}) %collective-permute-start.10) | collective-permute-done | bytes 65568 | tf_op jit(solution)/shard_map/ppermute | solution.py:522
  110.9 0.0 collective-permute-start.11
  110.9 5.9 %collective-permute-done.11 = f32[64,256]{1,0:T(8,128)S(1)} collective-permute-done((f32[64,256]{1,0:T(8,128)S(1)}, f32[64,256]{1,0:T(8,128)S(1)}, u32[]{:S(2)}, u32[]{:S(2)}) %collective-permute-start.11) | collective-permute-done | bytes 65568 | tf_op jit(solution)/shard_map/ppermute | solution.py:523
  116.8 0.0 collective-permute-start.12
  116.8 3.1 %collective-permute-start.16 = (f32[4,256,256]{2,1,0:T(8,128)S(1)}, f32[4,256,256]{2,1,0:T(8,128)S(1)}, u32[]{:S(2)}, u32[]{:S(2)}) collective-permute-start(f32[4,256,256]{2,1,0:T(8,128)S(1)} %add.21), channel_id=1, source_target_pairs={{0,8},{8,16},{16,24},{24,32},{32,40},{40,48},{48,56},{56,64},{64,7... | collective-permute-start | bytes 3145736 | tf_op jit(solution)/shard_map/ppermute | solution.py:507
  119.8 2.6 %collective-permute-done.12 = f32[64,256]{1,0:T(8,128)S(1)} collective-permute-done((f32[64,256]{1,0:T(8,128)S(1)}, f32[64,256]{1,0:T(8,128)S(1)}, u32[]{:S(2)}, u32[]{:S(2)}) %collective-permute-start.12) | collective-permute-done | bytes 65568 | tf_op jit(solution)/shard_map/ppermute | solution.py:524
  122.5 1.7 %collective-permute-start.13 = (f32[64,256]{1,0:T(8,128)S(1)}, f32[64,256]{1,0:T(8,128)S(1)}, u32[]{:S(2)}, u32[]{:S(2)}) collective-permute-start(f32[64,256]{1,0:T(8,128)S(1)} %add_add_fusion.1), channel_id=1, source_target_pairs={{0,24},{8,0},{16,8},{24,16},{32,56},{40,32},{48,40},{56,48},{64,88... | collective-permute-start | bytes 196616 | tf_op jit(solution)/shard_map/ppermute | solution.py:522
  124.1 2.6 %collective-permute-done.13 = f32[64,256]{1,0:T(8,128)S(1)} collective-permute-done((f32[64,256]{1,0:T(8,128)S(1)}, f32[64,256]{1,0:T(8,128)S(1)}, u32[]{:S(2)}, u32[]{:S(2)}) %collective-permute-start.13) | collective-permute-done | bytes 65568 | tf_op jit(solution)/shard_map/ppermute | solution.py:522
  126.8 2.8 %collective-permute-start.14 = (f32[64,256]{1,0:T(8,128)S(1)}, f32[64,256]{1,0:T(8,128)S(1)}, u32[]{:S(2)}, u32[]{:S(2)}) collective-permute-start(f32[64,256]{1,0:T(8,128)S(1)} %collective-permute-done.13), channel_id=1, source_target_pairs={{0,24},{8,0},{16,8},{24,16},{32,56},{40,32},{48,40},{56,48},{64,88... | collective-permute-start | bytes 196616 | tf_op jit(solution)/shard_map/ppermute | solution.py:523
  129.6 1.9 %collective-permute-done.14 = f32[64,256]{1,0:T(8,128)S(1)} collective-permute-done((f32[64,256]{1,0:T(8,128)S(1)}, f32[64,256]{1,0:T(8,128)S(1)}, u32[]{:S(2)}, u32[]{:S(2)}) %collective-permute-start.14) | collective-permute-done | bytes 65568 | tf_op jit(solution)/shard_map/ppermute | solution.py:523
  131.5 3.6 %collective-permute-start.15 = (f32[64,256]{1,0:T(8,128)S(1)}, f32[64,256]{1,0:T(8,128)S(1)}, u32[]{:S(2)}, u32[]{:S(2)}) collective-permute-start(f32[64,256]{1,0:T(8,128)S(1)} %collective-permute-done.14), channel_id=1, source_target_pairs={{0,24},{8,0},{16,8},{24,16},{32,56},{40,32},{48,40},{56,48},{64,88... | collective-permute-start | bytes 196616 | tf_op jit(solution)/shard_map/ppermute | solution.py:524
  135.1 0.0 collective-permute-done.7.refs_0_
  135.1 0.0 collective-permute-done.8.refs_1_
  135.1 3.8 %shard_map.98.base = f32[4,256,512]{2,1,0:T(8,128)} custom-call(f32[4,256,512]{2,1,0:T(8,128)} %get-tuple-element.26.base, f32[4,256,256]{2,1,0:T(8,128)S(1)} %collective-permute-done.7.refs_0_, f32[4,256,256]{2,1,0:T(8,128)S(1)} %collective-permute-done.8.refs_1_), custom_call_target="tpu_custom_call", output_to_operand_aliasing={{}: (0, {})} | custom-call | flops 524288 | bytes 4194304 | tf_op jit(solution)/shard_map/pallas_call | solution.py:492
  138.9 0.0 collective-permute-done.15
  139.0 13.2 %all_to_all.10 = f32[8,64,256]{2,1,0:T(8,128)S(1)} all-to-all(f32[8,64,256]{2,1,0:T(8,128)S(1)} %broadcast_in_dim.2), channel_id=1, replica_groups=mesh['row'=16,'col'=8] {'col'}, dimensions={0} | all-to-all | bytes 1048576 | tf_op jit(solution)/shard_map/all_to_all | solution.py:518
  152.2 0.0 collective-permute-done.16.refs_0_
  152.2 3.4 %shard_map.99 = f32[4,256,512]{2,1,0:T(8,128)} custom-call(f32[4,256,512]{2,1,0:T(8,128)} %shard_map.98.base, f32[4,256,256]{2,1,0:T(8,128)S(1)} %collective-permute-done.16.refs_0_), custom_call_target="tpu_custom_call", output_to_operand_aliasing={{}: (0, {})} | custom-call | flops 524288 | bytes 4194304 | tf_op jit(solution)/shard_map/pallas_call | solution.py:492
  155.6 0.8 copy.16
  (10 shorter events, 0.1 us)
Async XLA Ops:
  0.6 8.4 %copy-start = (f32[4,256,512]{2,1,0:T(8,128)S(1)}, f32[4,256,512]{2,1,0:T(8,128)}, u32[]{:S(2)}) copy-start(f32[4,256,512]{2,1,0:T(8,128)} %own.3) | copy-start | bytes 6291460
  3.7 11.0 %copy-start.10 = (s32[8,2]{0,1:T(2,128)S(1)}, s32[8,2]{0,1:T(2,128)}, u32[]{:S(2)}) copy-start(s32[8,2]{0,1:T(2,128)} %param.10) | copy-start | bytes 196
  3.7 11.1 %copy-start.2 = (f32[2,256,256]{2,1,0:T(8,128)S(1)}, f32[2,256,256]{2,1,0:T(8,128)}, u32[]{:S(2)}) copy-start(f32[2,256,256]{2,1,0:T(8,128)} %probe.1) | copy-start | bytes 1572868
  3.7 11.1 %copy-start.3 = (bf16[2,256,256]{2,1,0:T(8,128)(2,1)S(1)}, bf16[2,256,256]{2,1,0:T(8,128)(2,1)}, u32[]{:S(2)}) copy-start(bf16[2,256,256]{2,1,0:T(8,128)(2,1)} %constant.23.clone.fold) | copy-start | bytes 786436
  3.7 17.9 %collective-permute-start.1 = (f32[2,256,256]{2,1,0:T(8,128)}, f32[2,256,256]{2,1,0:T(8,128)S(1)}, u32[]{:S(2)}, u32[]{:S(2)}) collective-permute-start(f32[2,256,256]{2,1,0:T(8,128)} %get-tuple-element.39), channel_id=1, source_target_pairs={{8,0},{16,8},{24,16},{32,24},{40,32},{48,40},{56,48},{64,56},{72,6... | collective-permute-start | bytes 1572872 | tf_op jit(solution)/shard_map/ppermute | solution.py:507
  10.1 22.6 %collective-permute-start = (f32[4,256,256]{2,1,0:T(8,128)}, f32[4,256,256]{2,1,0:T(8,128)}, u32[]{:S(2)}, u32[]{:S(2)}) collective-permute-start(f32[4,256,256]{2,1,0:T(8,128)} %slice.23), channel_id=1, source_target_pairs={{1,0},{2,1},{3,2},{4,3},{5,4},{6,5},{7,6},{9,8},{10,9},{11,10},{12... | collective-permute-start | bytes 3145736 | tf_op jit(solution)/shard_map/ppermute | solution.py:507
  11.4 21.3 %collective-permute-start.3 = (f32[2,256,256]{2,1,0:T(8,128)}, f32[2,256,256]{2,1,0:T(8,128)}, u32[]{:S(2)}, u32[]{:S(2)}) collective-permute-start(f32[2,256,256]{2,1,0:T(8,128)} %get-tuple-element.36), channel_id=1, source_target_pairs={{8,0},{16,8},{24,16},{32,24},{40,32},{48,40},{56,48},{64,56},{72,6... | collective-permute-start | bytes 1572872 | tf_op jit(solution)/shard_map/ppermute | solution.py:507
  14.8 1.6 %copy-start.1 = (f32[8,256,256]{2,1,0:T(8,128)S(1)}, f32[8,256,256]{2,1,0:T(8,128)}, u32[]{:S(2)}) copy-start(f32[8,256,256]{2,1,0:T(8,128)} %amp.1) | copy-start | bytes 6291460
  16.4 6.5 %copy-start.9 = (f32[2,256,256]{2,1,0:T(8,128)S(1)}, f32[2,256,256]{2,1,0:T(8,128)}, u32[]{:S(2)}) copy-start(f32[2,256,256]{2,1,0:T(8,128)} %get-tuple-element.37) | copy-start | bytes 1572868
  16.4 12.9 %copy-start.8 = (f32[2,256,256]{2,1,0:T(8,128)S(1)}, f32[2,256,256]{2,1,0:T(8,128)}, u32[]{:S(2)}) copy-start(f32[2,256,256]{2,1,0:T(8,128)} %get-tuple-element.23) | copy-start | bytes 1572868
  16.4 16.3 %copy-start.6 = (bf16[12,256,256]{2,1,0:T(8,128)(2,1)S(1)}, bf16[12,256,256]{2,1,0:T(8,128)(2,1)}, u32[]{:S(2)}) copy-start(bf16[12,256,256]{2,1,0:T(8,128)(2,1)} %constant.21.clone.tab.hop_in) | copy-start | bytes 4718596
  20.1 19.0 %copy-start.4 = (f32[8,2,256,256]{3,2,1,0:T(8,128)}, f32[8,2,256,256]{3,2,1,0:T(8,128)S(1)}, u32[]{:S(2)}) copy-start(f32[8,2,256,256]{3,2,1,0:T(8,128)S(1)} %get-tuple-element.21.turned.turned_in) | copy-start | bytes 12582916
  20.1 19.0 %copy-start.5 = (f32[8,256,256]{2,1,0:T(8,128)}, f32[8,256,256]{2,1,0:T(8,128)S(1)}, u32[]{:S(2)}) copy-start(f32[8,256,256]{2,1,0:T(8,128)S(1)} %get-tuple-element.25.amp) | copy-start | bytes 6291460
  21.6 11.1 %collective-permute-start.4 = (f32[2,256,256]{2,1,0:T(8,128)S(1)}, f32[2,256,256]{2,1,0:T(8,128)S(1)}, u32[]{:S(2)}, u32[]{:S(2)}) collective-permute-start(f32[2,256,256]{2,1,0:T(8,128)S(1)} %collective-permute-done.1.down0.down0_one), channel_id=1, source_target_pairs={{1,0},{2,1},{3,2},{4,3},{5,4},{6,5},{7,6},{9,8},{10,9},{11,10},{12... | collective-permute-start | bytes 1572872 | tf_op jit(solution)/shard_map/ppermute | solution.py:507
  22.9 20.9 %collective-permute-start.2 = (f32[2,256,256]{2,1,0:T(8,128)S(1)}, f32[2,256,256]{2,1,0:T(8,128)S(1)}, u32[]{:S(2)}, u32[]{:S(2)}) collective-permute-start(f32[2,256,256]{2,1,0:T(8,128)S(1)} %copy-done.9), channel_id=1, source_target_pairs={{8,0},{16,8},{24,16},{32,24},{40,32},{48,40},{56,48},{64,56},{72,6... | collective-permute-start | bytes 1572872 | tf_op jit(solution)/shard_map/ppermute | solution.py:507
  29.4 24.7 %collective-permute-start.5 = (f32[2,256,256]{2,1,0:T(8,128)S(1)}, f32[2,256,256]{2,1,0:T(8,128)S(1)}, u32[]{:S(2)}, u32[]{:S(2)}) collective-permute-start(f32[2,256,256]{2,1,0:T(8,128)S(1)} %copy-done.8), channel_id=1, source_target_pairs={{8,0},{16,8},{24,16},{32,24},{40,32},{48,40},{56,48},{64,56},{72,6... | collective-permute-start | bytes 1572872 | tf_op jit(solution)/shard_map/ppermute | solution.py:507
  39.1 2.0 %copy-start.7 = (f32[8,2,256,256]{3,2,1,0:T(8,128)}, f32[8,2,256,256]{3,2,1,0:T(8,128)S(1)}, u32[]{:S(2)}) copy-start(f32[8,2,256,256]{3,2,1,0:T(8,128)S(1)} %shard_map.96.prop) | copy-start | bytes 12582916
  43.9 10.2 %collective-permute-start.6 = (f32[2,256,256]{2,1,0:T(8,128)S(1)}, f32[2,256,256]{2,1,0:T(8,128)S(1)}, u32[]{:S(2)}, u32[]{:S(2)}) collective-permute-start(f32[2,256,256]{2,1,0:T(8,128)S(1)} %collective-permute-done.2.down0_two), channel_id=1, source_target_pairs={{1,0},{2,1},{3,2},{4,3},{5,4},{6,5},{7,6},{9,8},{10,9},{11,10},{12... | collective-permute-start | bytes 1572872 | tf_op jit(solution)/shard_map/ppermute | solution.py:507
  70.9 32.8 %collective-permute-start.9 = (f32[4,256,256]{2,1,0:T(8,128)}, f32[4,256,256]{2,1,0:T(8,128)}, u32[]{:S(2)}, u32[]{:S(2)}) collective-permute-start(f32[4,256,256]{2,1,0:T(8,128)} %get-tuple-element.30), channel_id=1, source_target_pairs={{0,1},{1,2},{2,3},{3,4},{4,5},{5,6},{6,7},{8,9},{9,10},{10,11},{11... | collective-permute-start | bytes 3145736 | tf_op jit(solution)/shard_map/ppermute | solution.py:507
  74.3 29.3 %all-to-all-start = ((f32[8,64,256]{2,1,0:T(8,128)}), f32[8,64,256]{2,1,0:T(8,128)S(1)}, u32[]{:S(2)}, u32[]{:S(2)}) async-start(f32[8,64,256]{2,1,0:T(8,128)} %bitcast.2), calls=%async_computation | async-start | bytes 1048576 | tf_op jit(solution)/shard_map/all_to_all | solution.py:513
  88.9 46.2 %collective-permute-start.7 = (f32[4,256,256]{2,1,0:T(8,128)}, f32[4,256,256]{2,1,0:T(8,128)S(1)}, u32[]{:S(2)}, u32[]{:S(2)}) collective-permute-start(f32[4,256,256]{2,1,0:T(8,128)} %get-tuple-element.27), channel_id=1, source_target_pairs={{0,1},{1,2},{2,3},{3,4},{4,5},{5,6},{6,7},{8,9},{9,10},{10,11},{11... | collective-permute-start | bytes 3145736 | tf_op jit(solution)/shard_map/ppermute | solution.py:507
  91.4 43.7 %collective-permute-start.8 = (f32[4,256,256]{2,1,0:T(8,128)}, f32[4,256,256]{2,1,0:T(8,128)S(1)}, u32[]{:S(2)}, u32[]{:S(2)}) collective-permute-start(f32[4,256,256]{2,1,0:T(8,128)} %get-tuple-element.28), channel_id=1, source_target_pairs={{0,8},{8,16},{16,24},{24,32},{32,40},{40,48},{48,56},{56,64},{64,7... | collective-permute-start | bytes 3145736 | tf_op jit(solution)/shard_map/ppermute | solution.py:507
  105.4 5.5 %collective-permute-start.10 = (f32[64,256]{1,0:T(8,128)S(1)}, f32[64,256]{1,0:T(8,128)S(1)}, u32[]{:S(2)}, u32[]{:S(2)}) collective-permute-start(f32[64,256]{1,0:T(8,128)S(1)} %reduce_sum.9), channel_id=1, source_target_pairs={{0,96},{8,104},{16,112},{24,120},{32,0},{40,8},{48,16},{56,24},{64... | collective-permute-start | bytes 196616 | tf_op jit(solution)/shard_map/ppermute | solution.py:522
  110.9 5.9 %collective-permute-start.11 = (f32[64,256]{1,0:T(8,128)S(1)}, f32[64,256]{1,0:T(8,128)S(1)}, u32[]{:S(2)}, u32[]{:S(2)}) collective-permute-start(f32[64,256]{1,0:T(8,128)S(1)} %collective-permute-done.10), channel_id=1, source_target_pairs={{0,96},{8,104},{16,112},{24,120},{32,0},{40,8},{48,16},{56,24},{64... | collective-permute-start | bytes 196616 | tf_op jit(solution)/shard_map/ppermute | solution.py:523
  116.8 5.7 %collective-permute-start.12 = (f32[64,256]{1,0:T(8,128)S(1)}, f32[64,256]{1,0:T(8,128)S(1)}, u32[]{:S(2)}, u32[]{:S(2)}) collective-permute-start(f32[64,256]{1,0:T(8,128)S(1)} %collective-permute-done.11), channel_id=1, source_target_pairs={{0,96},{8,104},{16,112},{24,120},{32,0},{40,8},{48,16},{56,24},{64... | collective-permute-start | bytes 196616 | tf_op jit(solution)/shard_map/ppermute | solution.py:524
  116.8 35.4 %collective-permute-start.16 = (f32[4,256,256]{2,1,0:T(8,128)S(1)}, f32[4,256,256]{2,1,0:T(8,128)S(1)}, u32[]{:S(2)}, u32[]{:S(2)}) collective-permute-start(f32[4,256,256]{2,1,0:T(8,128)S(1)} %add.21), channel_id=1, source_target_pairs={{0,8},{8,16},{16,24},{24,32},{32,40},{40,48},{48,56},{56,64},{64,7... | collective-permute-start | bytes 3145736 | tf_op jit(solution)/shard_map/ppermute | solution.py:507
  122.5 4.3 %collective-permute-start.13 = (f32[64,256]{1,0:T(8,128)S(1)}, f32[64,256]{1,0:T(8,128)S(1)}, u32[]{:S(2)}, u32[]{:S(2)}) collective-permute-start(f32[64,256]{1,0:T(8,128)S(1)} %add_add_fusion.1), channel_id=1, source_target_pairs={{0,24},{8,0},{16,8},{24,16},{32,56},{40,32},{48,40},{56,48},{64,88... | collective-permute-start | bytes 196616 | tf_op jit(solution)/shard_map/ppermute | solution.py:522
  126.8 4.7 %collective-permute-start.14 = (f32[64,256]{1,0:T(8,128)S(1)}, f32[64,256]{1,0:T(8,128)S(1)}, u32[]{:S(2)}, u32[]{:S(2)}) collective-permute-start(f32[64,256]{1,0:T(8,128)S(1)} %collective-permute-done.13), channel_id=1, source_target_pairs={{0,24},{8,0},{16,8},{24,16},{32,56},{40,32},{48,40},{56,48},{64,88... | collective-permute-start | bytes 196616 | tf_op jit(solution)/shard_map/ppermute | solution.py:523
  131.5 7.4 %collective-permute-start.15 = (f32[64,256]{1,0:T(8,128)S(1)}, f32[64,256]{1,0:T(8,128)S(1)}, u32[]{:S(2)}, u32[]{:S(2)}) collective-permute-start(f32[64,256]{1,0:T(8,128)S(1)} %collective-permute-done.14), channel_id=1, source_target_pairs={{0,24},{8,0},{16,8},{24,16},{32,56},{40,32},{48,40},{56,48},{64,88... | collective-permute-start | bytes 196616 | tf_op jit(solution)/shard_map/ppermute | solution.py:524

commit v3 on v2

--- a/solution.py
+++ b/solution.py
@@ -313,9 +313,9 @@
             put(f, prop, u)
 
 
-def second_kernel(meta, own, right, down0_one, down0_two, down1_one, corner_one, turned_in, hop_in, down1_two, corner_two,
-                  prop, amp, dft, gown, gright, gdown0, gdown1, gcorner, gprobe,
-                  ext, gext, acc, turned, hop, win, sems):
+def second_kernel(meta, own, right, down0_one, down0_two, down1_one, corner_one, turned_in, hop_in, prop_in, amp_in,
+                  down1_two, corner_two, dft, gown, gright, gdown0, gdown1, gcorner, gprobe,
+                  ext, gext, acc, turned, hop, prop, amp, win, sems):
     step = pl.program_id(0)
     group = range(GROUP)
     one, two = pl.ds(0, 2), pl.ds(2, 2)
@@ -323,13 +323,21 @@
     refs_two = (own.at[two], right.at[two], down0_two, down1_two, corner_two)
     copies_one = tile_copies(refs_one, ext.at[:, one], sems.at[0])
     copies_two = tile_copies(refs_two, ext.at[:, two], sems.at[1])
-    copy_turned = (turned_in, turned, sems.at[2, 0])
-    copy_hop = (hop_in, hop, sems.at[2, 1])
+    now, later = pl.ds(0, GROUP), pl.ds(GROUP, SLOTS - GROUP)
+    copies_now = copies_two + [
+        (prop_in.at[now], prop.at[now], sems.at[2, 0]),
+        (amp_in.at[now], amp.at[now], sems.at[2, 1]),
+    ]
+    copies_later = [(hop_in, hop, sems.at[2, 2])] + copies_one + [
+        (turned_in, turned, sems.at[2, 3]),
+        (prop_in.at[later], prop.at[later], sems.at[2, 4]),
+        (amp_in.at[later], amp.at[later], sems.at[2, 5]),
+    ]
 
     @pl.when(step == 0)
     def begin():
-        started = start_copies(copies_two)
-        start_copies([copy_hop] + copies_one + [copy_turned])
+        started = start_copies(copies_now)
+        start_copies(copies_later)
         gext[...] = jnp.zeros_like(gext)
         acc[...] = jnp.zeros_like(acc)
         wait_copies(started)
@@ -340,40 +348,41 @@
     def stage_one():
         for u in group:
             load_window(meta, step * GROUP + u, ext, (2, 3), win, u)
-        fields = [times(pair(prop, u), (win[u, 2], win[u, 3])) for u in group]
+        fields = [times(pair(prop, step * GROUP + u), (win[u, 2], win[u, 3])) for u in group]
         fields = [spread_left(half_left(f, dft, 1)) for f in fields]
         fields = [spread_right(half_right(f, dft, 0)) for f in fields]
         chi = []
         for u, f in enumerate(fields):
-            factor = 1.0 - amp[u] * lax.rsqrt(f[0] * f[0] + f[1] * f[1] + 1.0)
+            factor = 1.0 - amp[step * GROUP + u] * lax.rsqrt(f[0] * f[0] + f[1] * f[1] + 1.0)
             chi.append((factor * f[0], factor * f[1]))
         fields = [half_right(gather_right(f), dft, 1) for f in chi]
         fields = [half_left(gather_left(f), dft, 0) for f in fields]
         waves = [conj_times((win[u, 2], win[u, 3]), f) for u, f in enumerate(fields)]
         for u, f in enumerate(fields):
-            win[u, 2], win[u, 3] = conj_times(pair(prop, u), f)
+            win[u, 2], win[u, 3] = conj_times(pair(prop, step * GROUP + u), f)
         for u, f in enumerate(waves):
-            put(f, prop, u)
+            put(f, prop, step * GROUP + u)
 
     @pl.when(step == 0)
     def arrive():
-        wait_copies([pltpu.make_async_copy(*copy) for copy in [copy_hop] + copies_one + [copy_turned]])
+        wait_copies([pltpu.make_async_copy(*copy) for copy in copies_later])
 
     @pl.when(live)
     def stage_two():
         for u in group:
             load_window(meta, step * GROUP + u, ext, (0, 1), win, u)
-        waves = [hop_left(pair(prop, u), hop, 0, True) for u in group]
+            add_window(meta, step * GROUP + u, win, u, (2, 3), gext)
+        waves = [hop_left(pair(prop, step * GROUP + u), hop, 0, True) for u in group]
         waves = [hop_right(f, hop, 1, True) for f in waves]
         for u, wave in enumerate(waves):
             probe = pair(turned, step * GROUP + u)
             grad, part = conj_times(probe, wave), conj_times(pair(win, u), wave)
             put(grad, win, u)
-            put(part, prop, u)
+            put(part, prop, step * GROUP + u)
 
         def finish(slot, u):
-            add_window(meta, slot, win, u, range(4), gext)
-            add_probe(meta, slot, prop, u, acc)
+            add_window(meta, slot, win, u, (0, 1), gext)
+            add_probe(meta, slot, prop, slot, acc)
 
         for u in group:
             slot = step * GROUP + u
@@ -454,7 +463,7 @@
             pltpu.SemaphoreType.DMA((5,)),
         ],
         24,
-        32,
+        52,
     )(*args)
 
 
@@ -462,7 +471,7 @@
     return call(
         second_kernel,
         SLOTS // GROUP,
-        [SCALARS] + [ANYWHERE] * 8 + [WHOLE, WHOLE, FIELDS, PLANES, WHOLE],
+        [SCALARS] + [ANYWHERE] * 10 + [WHOLE] * 3,
         [ANYWHERE] * 5 + [WHOLE],
         [shape(4, W, TC)] + [shape(4, W, W)] * 4 + [shape(2, W, W)],
         [
@@ -471,34 +480,34 @@
             pltpu.VMEM((2, 2, 2 * W, HALF_W), F32),
             pltpu.VMEM((SLOTS, 2, W, W), F32),
             pltpu.VMEM((12, W, W), BF16),
+            pltpu.VMEM((SLOTS, 2, W, W), F32),
+            pltpu.VMEM((SLOTS, W, W), F32),
             pltpu.VMEM((GROUP, 4, W, W), F32),
-            pltpu.SemaphoreType.DMA((3, 5)),
+            pltpu.SemaphoreType.DMA((3, 6)),
         ],
         48,
         50,
     )(*args)
 
 
-def add_kernel(base, *refs):
-    parts, out = refs[:-1], refs[-1]
-    for i, part in enumerate(parts):
-        here = pl.ds(i * W, W)
-        out[:, :, here] = base[:, :, here] + part[...]
-
-
-def add_call(base, *parts):
-    block = pl.BlockSpec((1, W, W * len(parts)), lambda i: (i, 0, 0))
+def add_kernel(base, right, down0, down1, out):
+    first, second = pl.ds(0, W), pl.ds(W, W)
+    out[:, :, first] = base[:, :, first] + (right[...] + down0[...])
+    out[:, :, second] = base[:, :, second] + down1[...]
+
+
+def add_call(*args):
+    whole = pl.BlockSpec((1, W, TC), lambda i: (i, 0, 0))
     part = pl.BlockSpec((1, W, W), lambda i: (i, 0, 0))
     return pl.pallas_call(
         add_kernel,
         grid=(4,),
-        in_specs=[block] + [part] * len(parts),
-        out_specs=block,
+        in_specs=[whole] + [part] * 3,
+        out_specs=whole,
         out_shape=shape(4, W, TC),
-        input_output_aliases={0: 0},
         compiler_params=pltpu.CompilerParams(vmem_limit_bytes=8 * 2**20),
-        cost_estimate=pl.CostEstimate(flops=2**19, bytes_accessed=2**22, transcendentals=0),
-    )(base, *parts)
+        cost_estimate=pl.CostEstimate(flops=2**20, bytes_accessed=7 * 2**20, transcendentals=0),
+    )(*args)
 
 
 def shift(value, axis, steps):
@@ -531,20 +540,21 @@
     local_cols = scan_offsets[:, 1] - lax.axis_index("col") * cols_tile
     meta = jnp.concatenate([live_counts, local_rows, local_cols])
     hop, dft, fold = jnp.asarray(hop_tables()), jnp.asarray(dft_tables()), jnp.asarray(fold_tables())
-    down0_one = shift(object_slab[:2, :, :W], "row", -1)
-    down1_one = shift(object_slab[:2, :, W:], "row", -1)
-    right = shift(object_slab[:, :, :W], "col", -1)
-    down0_two = shift(object_slab[2:, :, :W], "row", -1)
+    first_part, rest = lax.optimization_barrier((object_slab[:2, :, :W], object_slab))
+    down0_one = shift(first_part, "row", -1)
+    down1_one = shift(rest[:2, :, W:], "row", -1)
+    right = shift(rest[:, :, :W], "col", -1)
+    down0_two = shift(rest[2:, :, :W], "row", -1)
     amp, turned = prepare_call(meta, probe_wave, amplitudes, fold)
-    down0_one, turned, last_part = lax.optimization_barrier((down0_one, turned, object_slab[2:, :, W:]))
+    down0_one, turned, last_part = lax.optimization_barrier((down0_one, turned, rest[2:, :, W:]))
     corner_one = shift(down0_one, "col", -1)
     down1_two = shift(last_part, "row", -1)
     prop = first_call(meta, object_slab, right, down0_one, down1_one, corner_one, turned, hop)
     down0_two, prop = lax.optimization_barrier((down0_two, prop))
     corner_two = shift(down0_two, "col", -1)
     gown, gright, gdown0, gdown1, gcorner, gprobe = second_call(
-        meta, object_slab, right, down0_one, down0_two, down1_one, corner_one, turned, hop, down1_two, corner_two,
-        prop, amp, dft,
+        meta, object_slab, right, down0_one, down0_two, down1_one, corner_one, turned, hop, prop, amp,
+        down1_two, corner_two, dft,
     )
     side = lax.axis_size("row") // 4
     to_left_x = [(i, (i - side) % (4 * side)) for i in range(4 * side)]
@@ -552,13 +562,11 @@
     corner_back = shift(gcorner, "col", 1)
     down1_back = shift(gdown1, "row", 1)
     share = add_shares(gprobe, "col")
-    gdown0, share = lax.optimization_barrier((gdown0 + corner_back, share))
-    down0_back = shift(gdown0, "row", 1)
+    down0_back = shift(gdown0 + corner_back, "row", 1)
     right_back = shift(gright, "col", 1)
     share = ring_sum(ring_sum(share, to_left_x), to_left_y)
-    gown, share = lax.optimization_barrier((add_call(gown, right_back, down1_back), share))
     probe_grad = hand_out(share, "col").reshape(probe_wave.shape)
-    return add_call(gown, down0_back), probe_grad
+    return add_call(gown, right_back, down0_back, down1_back), probe_grad
 
 
 def solution(mesh):

time: 157 us -> 170 us (1.083); the launches traced: 156 us -> 171 us
  blocking collectives: 13.2 us -> 46.3 us
  starting transfers between devices: 55.8 us -> 32.7 us
  waiting for transfers between devices: 41.5 us -> 51.5 us
  Pallas kernels: 34 us -> 30.6 us
    all_to_all x0 -> x1, blocking collectives: none -> 33 us  [add_shares(): return lax.all_to_all(shares, axis, 0, 0, tiled=True).sum(axis=0)]
    ppermute x11, waiting for transfers between devices: 14.5 us -> 31.2 us  [shift(): lax.ppermute(value, axis, [(source, source + steps) for source in range(f...]
    all_to_all x1 -> x0, starting transfers between devices: 14.6 us -> none  [add_shares(): return lax.all_to_all(shares, axis, 0, 0, tiled=True).sum(axis=0)]
    all_to_all x1 -> x0, waiting for transfers between devices: 9.08 us -> none  [add_shares(): return lax.all_to_all(shares, axis, 0, 0, tiled=True).sum(axis=0)]
    pallas_call x3 -> x2, Pallas kernels: 24 us -> 17.4 us  [the longest x1 15.4 us: second_call(): call(second_kernel, SLOTS // GROUP, [SCALARS] + [ANYWHERE] * 10 + [WHOLE]...]
    ppermute x11, starting transfers between devices: 32.5 us -> 28.5 us  [shift(): lax.ppermute(value, axis, [(source, source + steps) for source in range(f...]
    pallas_call x1, Pallas kernels: 6.37 us -> 9.59 us  [first_call(): call(first_kernel, SLOTS // GROUP, [SCALARS] + [ANYWHERE] * 3 + [WHOLE, W...]
    ppermute x2, waiting for transfers between devices: 7.6 us -> 9.84 us  [ring_sum(): first = lax.ppermute(value, 'row', pairs)]
  transfers between devices with their start and end apart: 18 -> 17, of which waited for: 10 -> 9; matrix products, arithmetic and copies ran while one was open for 2% -> 2% of each run, Pallas kernels for 9% -> 8%
where the time goes in v3:
time: 170 us; the launch traced here: 171 us
  waiting for transfers between devices  51.5 us (30%)
  blocking collectives  46.3 us (27%)
  starting transfers between devices  32.7 us (19%)
  Pallas kernels  30.6 us (18%)
  local copies, waits for them, and re-layouts  8.44 us (5%)
    all_to_all x1, blocking collectives, add_shares(): return lax.all_to_all(shares, axis, 0, 0, tiled=True).sum(axis=0)  33 us
    ppermute x11, waiting for transfers between devices, shift(): lax.ppermute(value, axis, [(source, source + steps) for source in range(f...  31.2 us
    ppermute x11, starting transfers between devices, shift(): lax.ppermute(value, axis, [(source, source + steps) for source in range(f...  28.5 us
    pallas_call x1, Pallas kernels, second_call(): call(second_kernel, SLOTS // GROUP, [SCALARS] + [ANYWHERE] * 10 + [WHOLE]...  15.4 us
    all_to_all x1, blocking collectives, hand_out(): return lax.all_to_all(spread, axis, 0, 0, tiled=True)  13.3 us
    ppermute x2, waiting for transfers between devices, ring_sum(): first = lax.ppermute(value, 'row', pairs)  9.84 us
    pallas_call x1, Pallas kernels, first_call(): call(first_kernel, SLOTS // GROUP, [SCALARS] + [ANYWHERE] * 3 + [WHOLE, W...  9.59 us
    ppermute x2, waiting for transfers between devices, ring_sum(): second = lax.ppermute(first, 'row', pairs)  8.52 us
  transfers between devices with their start and end apart: 17, of which 9 were waited for; matrix products, arithmetic and copies ran while one was open for 2% of the time, Pallas kernels for 8%

profile of v3, /device:TPU:6, one launch (start us, length us, event | category | flops | bytes accessed | tf_op | source)
XLA Modules:
  0.0 171.4 jit_solution(9530452836892339174)
XLA Ops:
  0.6 0.0 copy-start.6
  0.6 2.0 %slice.23 = f32[2,256,256]{2,1,0:T(8,128)} slice(f32[4,256,512]{2,1,0:T(8,128)} %own.3), slice={[0:2], [0:256], [0:256]} | slice | bytes 1048576 | tf_op jit(solution)/shard_map/slice | solution.py:543
  2.7 5.2 %collective-permute-start.1 = (f32[2,256,256]{2,1,0:T(8,128)}, f32[2,256,256]{2,1,0:T(8,128)S(1)}, u32[]{:S(2)}, u32[]{:S(2)}) collective-permute-start(f32[2,256,256]{2,1,0:T(8,128)} %slice.23), channel_id=1, source_target_pairs={{8,0},{16,8},{24,16},{32,24},{40,32},{48,40},{56,48},{64,56},{72,6... | collective-permute-start | bytes 1572872 | tf_op jit(solution)/shard_map/ppermute | solution.py:516
  7.8 2.3 %slice.24 = f32[4,256,256]{2,1,0:T(8,128)} slice(f32[4,256,512]{2,1,0:T(8,128)} %own.3), slice={[0:4], [0:256], [0:256]} | slice | bytes 2097152 | tf_op jit(solution)/shard_map/slice | solution.py:546
  10.2 0.0 copy-start.10
  10.2 1.6 collective-permute-start
  11.7 0.0 copy-done.6
  11.8 1.3 fusion
  13.0 2.6 %collective-permute-start.3 = (f32[2,256,256]{2,1,0:T(8,128)}, f32[2,256,256]{2,1,0:T(8,128)}, u32[]{:S(2)}, u32[]{:S(2)}) collective-permute-start(f32[2,256,256]{2,1,0:T(8,128)} %get-tuple-element.32), channel_id=1, source_target_pairs={{8,0},{16,8},{24,16},{32,24},{40,32},{48,40},{56,48},{64,56},{72,6... | collective-permute-start | bytes 1572872 | tf_op jit(solution)/shard_map/ppermute | solution.py:516
  16.3 0.0 copy-done.10
  16.3 0.0 copy-start.9
  16.3 0.0 copy-start.8
  16.4 0.1 pad_add_fusion.meta
  16.4 0.0 copy-done.1
  16.5 0.0 copy-done.2
  16.5 0.0 copy-done.3
  16.5 3.7 %shard_map.95 = (f32[8,256,256]{2,1,0:T(8,128)S(1)}, f32[8,2,256,256]{3,2,1,0:T(8,128)S(1)}) custom-call(s32[17]{0:T(128)S(1)} %pad_add_fusion.meta, f32[2,256,256]{2,1,0:T(8,128)S(1)} %copy-done.2, f32[8,256,256]{2,1,0:T(8,128)S(1)} %copy-done.1, bf16[2,256,256]{2,1,0:T(8,128)(2,1)S(1)} %copy-done.3), custom_call_target="tpu_custom_call" | custom-call | tf_op jit(solution)/shard_map/pallas_call | solution.py:438
  20.1 0.0 copy-start.4
  20.2 1.9 %copy-done.4 = f32[8,2,256,256]{3,2,1,0:T(8,128)} copy-done((f32[8,2,256,256]{3,2,1,0:T(8,128)}, f32[8,2,256,256]{3,2,1,0:T(8,128)S(1)}, u32[]{:S(2)}) %copy-start.4) | copy-done | bytes 4194328
  22.1 0.0 collective-permute-done.1.down0.down0_one
  22.1 1.3 collective-permute-start.4
  23.4 0.0 copy-done.9
  23.4 4.7 %collective-permute-start.2 = (f32[2,256,256]{2,1,0:T(8,128)S(1)}, f32[2,256,256]{2,1,0:T(8,128)S(1)}, u32[]{:S(2)}, u32[]{:S(2)}) collective-permute-start(f32[2,256,256]{2,1,0:T(8,128)S(1)} %copy-done.9), channel_id=1, source_target_pairs={{8,0},{16,8},{24,16},{32,24},{40,32},{48,40},{56,48},{64,56},{72,6... | collective-permute-start | bytes 1572872 | tf_op jit(solution)/shard_map/ppermute | solution.py:516
  28.2 0.0 copy-done.8
  28.2 1.9 %collective-permute-start.5 = (f32[2,256,256]{2,1,0:T(8,128)S(1)}, f32[2,256,256]{2,1,0:T(8,128)S(1)}, u32[]{:S(2)}, u32[]{:S(2)}) collective-permute-start(f32[2,256,256]{2,1,0:T(8,128)S(1)} %copy-done.8), channel_id=1, source_target_pairs={{8,0},{16,8},{24,16},{32,24},{40,32},{48,40},{56,48},{64,56},{72,6... | collective-permute-start | bytes 1572872 | tf_op jit(solution)/shard_map/ppermute | solution.py:516
  30.1 1.4 collective-permute-done.3.down1.down1_one
  31.6 0.0 collective-permute-done.right
  31.6 0.0 collective-permute-done.4.corner.corner_one
  31.6 9.6 %shard_map.96.prop_in = f32[8,2,256,256]{3,2,1,0:T(8,128)} custom-call(s32[17]{0:T(128)S(1)} %pad_add_fusion.meta, f32[4,256,512]{2,1,0:T(8,128)} %own.3, f32[4,256,256]{2,1,0:T(8,128)} %collective-permute-done.right, f32[2,256,256]{2,1,0:T(8,128)S(1)} %collective-permute-done.1.down0.down0_one, f32[2,256,256]{2,1,0:T(8,128)} %collective-permute-done.3.down1.down1_one, ...), custom_call_target="tpu_custom_call" | custom-call | flops 6442450944 | bytes 6291456 | tf_op jit(solution)/shard_map/pallas_call | solution.py:454
  41.2 0.0 copy-done.5
  41.2 1.5 collective-permute-done.2.down0_two
  42.7 1.5 collective-permute-start.6
  44.1 8.8 %collective-permute-done.5.down1_two = f32[2,256,256]{2,1,0:T(8,128)S(1)} collective-permute-done((f32[2,256,256]{2,1,0:T(8,128)S(1)}, f32[2,256,256]{2,1,0:T(8,128)S(1)}, u32[]{:S(2)}, u32[]{:S(2)}) %collective-permute-start.5) | collective-permute-done | bytes 524320 | tf_op jit(solution)/shard_map/ppermute | solution.py:516
  52.9 0.0 collective-permute-done.6.corner_two
  52.9 15.4 %shard_map.97 = (f32[4,256,512]{2,1,0:T(8,128)}, f32[4,256,256]{2,1,0:T(8,128)}, f32[4,256,256]{2,1,0:T(8,128)}, f32[4,256,256]{2,1,0:T(8,128)}, f32[4,256,256]{2,1,0:T(8,128)}, /*index=5*/f32[2,256,256]{2,1,0:T(8,128)S(1)}) custom-call(s32[17]{0:T(128)S(1)} %pad_add_fusion.meta, f32[4,256,512]{2,1,0:T(8,128)} %own.3, ...), custom_call_target="tpu_custom_call" | custom-call | flops 12884901888 | bytes 12582912 | tf_op jit(solution)/shard_map/pallas_call | solution.py:471
  68.4 0.0 copy-start.7
  68.4 3.1 %collective-permute-start.8 = (f32[4,256,256]{2,1,0:T(8,128)}, f32[4,256,256]{2,1,0:T(8,128)S(1)}, u32[]{:S(2)}, u32[]{:S(2)}) collective-permute-start(f32[4,256,256]{2,1,0:T(8,128)} %get-tuple-element.29), channel_id=1, source_target_pairs={{0,1},{1,2},{2,3},{3,4},{4,5},{5,6},{6,7},{8,9},{9,10},{10,11},{11... | collective-permute-start | bytes 3145736 | tf_op jit(solution)/shard_map/ppermute | solution.py:516
  71.5 33.0 %all_to_all.10 = f32[8,64,256]{2,1,0:T(8,128)S(1)} all-to-all(f32[8,64,256]{2,1,0:T(8,128)S(1)} %bitcast.6), channel_id=1, replica_groups=mesh['row'=16,'col'=8] {'col'}, dimensions={0} | all-to-all | bytes 1048576 | tf_op jit(solution)/shard_map/all_to_all | solution.py:522
  104.5 0.6 collective-permute-start.11
  105.1 5.6 %collective-permute-done.11 = f32[64,256]{1,0:T(8,128)S(1)} collective-permute-done((f32[64,256]{1,0:T(8,128)S(1)}, f32[64,256]{1,0:T(8,128)S(1)}, u32[]{:S(2)}, u32[]{:S(2)}) %collective-permute-start.11) | collective-permute-done | bytes 65568 | tf_op jit(solution)/shard_map/ppermute | solution.py:531
  110.7 0.0 collective-permute-start.12
  110.7 5.5 %collective-permute-done.12 = f32[64,256]{1,0:T(8,128)S(1)} collective-permute-done((f32[64,256]{1,0:T(8,128)S(1)}, f32[64,256]{1,0:T(8,128)S(1)}, u32[]{:S(2)}, u32[]{:S(2)}) %collective-permute-start.12) | collective-permute-done | bytes 65568 | tf_op jit(solution)/shard_map/ppermute | solution.py:532
  116.2 0.0 collective-permute-start.13
  116.2 1.3 collective-permute-start.7
  117.5 3.2 %collective-permute-start.10 = (f32[4,256,256]{2,1,0:T(8,128)}, f32[4,256,256]{2,1,0:T(8,128)S(1)}, u32[]{:S(2)}, u32[]{:S(2)}) collective-permute-start(f32[4,256,256]{2,1,0:T(8,128)} %get-tuple-element.30), channel_id=1, source_target_pairs={{0,8},{8,16},{16,24},{24,32},{32,40},{40,48},{48,56},{56,64},{64,7... | collective-permute-start | bytes 3145736 | tf_op jit(solution)/shard_map/ppermute | solution.py:516
  120.7 0.0 collective-permute-done.8
  120.7 0.0 copy-done.7
  120.7 0.0 copy-start
  120.7 0.1 add.21
  120.9 2.1 %collective-permute-start.9 = (f32[4,256,256]{2,1,0:T(8,128)S(1)}, f32[4,256,256]{2,1,0:T(8,128)S(1)}, u32[]{:S(2)}, u32[]{:S(2)}) collective-permute-start(f32[4,256,256]{2,1,0:T(8,128)S(1)} %add.21), channel_id=1, source_target_pairs={{0,8},{8,16},{16,24},{24,32},{32,40},{40,48},{48,56},{56,64},{64,7... | collective-permute-start | bytes 3145736 | tf_op jit(solution)/shard_map/ppermute | solution.py:516
  122.9 0.0 collective-permute-done.13
  122.9 0.1 collective-permute-start.14
  123.0 4.3 %collective-permute-done.14 = f32[64,256]{1,0:T(8,128)S(1)} collective-permute-done((f32[64,256]{1,0:T(8,128)S(1)}, f32[64,256]{1,0:T(8,128)S(1)}, u32[]{:S(2)}, u32[]{:S(2)}) %collective-permute-start.14) | collective-permute-done | bytes 65568 | tf_op jit(solution)/shard_map/ppermute | solution.py:531
  127.3 1.2 collective-permute-start.15
  128.5 3.0 %collective-permute-done.15 = f32[64,256]{1,0:T(8,128)S(1)} collective-permute-done((f32[64,256]{1,0:T(8,128)S(1)}, f32[64,256]{1,0:T(8,128)S(1)}, u32[]{:S(2)}, u32[]{:S(2)}) %collective-permute-start.15) | collective-permute-done | bytes 65568 | tf_op jit(solution)/shard_map/ppermute | solution.py:532
  131.6 2.4 %collective-permute-start.16 = (f32[64,256]{1,0:T(8,128)S(1)}, f32[64,256]{1,0:T(8,128)S(1)}, u32[]{:S(2)}, u32[]{:S(2)}) collective-permute-start(f32[64,256]{1,0:T(8,128)S(1)} %collective-permute-done.15), channel_id=1, source_target_pairs={{0,24},{8,0},{16,8},{24,16},{32,56},{40,32},{48,40},{56,48},{64,88... | collective-permute-start | bytes 196616 | tf_op jit(solution)/shard_map/ppermute | solution.py:533
  134.0 1.9 %collective-permute-done.16 = f32[64,256]{1,0:T(8,128)S(1)} collective-permute-done((f32[64,256]{1,0:T(8,128)S(1)}, f32[64,256]{1,0:T(8,128)S(1)}, u32[]{:S(2)}, u32[]{:S(2)}) %collective-permute-start.16) | collective-permute-done | bytes 65568 | tf_op jit(solution)/shard_map/ppermute | solution.py:533
  135.9 13.3 %all_to_all.11 = f32[8,64,256]{2,1,0:T(8,128)S(1)} all-to-all(f32[8,64,256]{2,1,0:T(8,128)S(1)} %broadcast_in_dim.2), channel_id=1, replica_groups=mesh['row'=16,'col'=8] {'col'}, dimensions={0} | all-to-all | bytes 1048576 | tf_op jit(solution)/shard_map/all_to_all | solution.py:527
  149.2 0.0 collective-permute-done.7.right
  149.2 0.0 collective-permute-done.10.down1
  149.3 19.4 %collective-permute-done.9.down0 = f32[4,256,256]{2,1,0:T(8,128)S(1)} collective-permute-done((f32[4,256,256]{2,1,0:T(8,128)S(1)}, f32[4,256,256]{2,1,0:T(8,128)S(1)}, u32[]{:S(2)}, u32[]{:S(2)}) %collective-permute-start.9) | collective-permute-done | bytes 1048608 | tf_op jit(solution)/shard_map/ppermute | solution.py:516
  168.7 0.0 copy-done
  168.7 1.9 %shard_map.98 = f32[4,256,512]{2,1,0:T(8,128)} custom-call(f32[4,256,512]{2,1,0:T(8,128)S(1)} %copy-done, f32[4,256,256]{2,1,0:T(8,128)S(1)} %collective-permute-done.7.right, f32[4,256,256]{2,1,0:T(8,128)S(1)} %collective-permute-done.9.down0, f32[4,256,256]{2,1,0:T(8,128)S(1)} %collective-permute-done.10.down1), custom_call_target="tpu_custom_call" | custom-call | flops 1048576 | bytes 7340032 | tf_op jit(solution)/shard_map/pallas_call | solution.py:502
  170.6 0.8 copy.12
  (9 shorter events, 0.1 us)
Async XLA Ops:
  0.6 11.1 %copy-start.6 = (f32[4,256,512]{2,1,0:T(8,128)S(1)}, f32[4,256,512]{2,1,0:T(8,128)}, u32[]{:S(2)}) copy-start(f32[4,256,512]{2,1,0:T(8,128)} %own.3) | copy-start | bytes 6291460
  2.7 19.4 %collective-permute-start.1 = (f32[2,256,256]{2,1,0:T(8,128)}, f32[2,256,256]{2,1,0:T(8,128)S(1)}, u32[]{:S(2)}, u32[]{:S(2)}) collective-permute-start(f32[2,256,256]{2,1,0:T(8,128)} %slice.23), channel_id=1, source_target_pairs={{8,0},{16,8},{24,16},{32,24},{40,32},{48,40},{56,48},{64,56},{72,6... | collective-permute-start | bytes 1572872 | tf_op jit(solution)/shard_map/ppermute | solution.py:516
  10.2 6.2 %copy-start.10 = (s32[8,2]{0,1:T(2,128)S(1)}, s32[8,2]{0,1:T(2,128)}, u32[]{:S(2)}) copy-start(s32[8,2]{0,1:T(2,128)} %param.10) | copy-start | bytes 196
  10.2 6.3 %copy-start.1 = (f32[8,256,256]{2,1,0:T(8,128)S(1)}, f32[8,256,256]{2,1,0:T(8,128)}, u32[]{:S(2)}) copy-start(f32[8,256,256]{2,1,0:T(8,128)} %amp.1) | copy-start | bytes 6291460
  10.2 6.3 %copy-start.2 = (f32[2,256,256]{2,1,0:T(8,128)S(1)}, f32[2,256,256]{2,1,0:T(8,128)}, u32[]{:S(2)}) copy-start(f32[2,256,256]{2,1,0:T(8,128)} %probe.1) | copy-start | bytes 1572868
  10.2 6.3 %copy-start.3 = (bf16[2,256,256]{2,1,0:T(8,128)(2,1)S(1)}, bf16[2,256,256]{2,1,0:T(8,128)(2,1)}, u32[]{:S(2)}) copy-start(bf16[2,256,256]{2,1,0:T(8,128)(2,1)} %constant.23.clone.fold) | copy-start | bytes 786436
  10.2 21.4 %collective-permute-start = (f32[4,256,256]{2,1,0:T(8,128)}, f32[4,256,256]{2,1,0:T(8,128)}, u32[]{:S(2)}, u32[]{:S(2)}) collective-permute-start(f32[4,256,256]{2,1,0:T(8,128)} %slice.24), channel_id=1, source_target_pairs={{1,0},{2,1},{3,2},{4,3},{5,4},{6,5},{7,6},{9,8},{10,9},{11,10},{12... | collective-permute-start | bytes 3145736 | tf_op jit(solution)/shard_map/ppermute | solution.py:516
  13.0 18.5 %collective-permute-start.3 = (f32[2,256,256]{2,1,0:T(8,128)}, f32[2,256,256]{2,1,0:T(8,128)}, u32[]{:S(2)}, u32[]{:S(2)}) collective-permute-start(f32[2,256,256]{2,1,0:T(8,128)} %get-tuple-element.32), channel_id=1, source_target_pairs={{8,0},{16,8},{24,16},{32,24},{40,32},{48,40},{56,48},{64,56},{72,6... | collective-permute-start | bytes 1572872 | tf_op jit(solution)/shard_map/ppermute | solution.py:516
  16.3 7.1 %copy-start.9 = (f32[2,256,256]{2,1,0:T(8,128)S(1)}, f32[2,256,256]{2,1,0:T(8,128)}, u32[]{:S(2)}) copy-start(f32[2,256,256]{2,1,0:T(8,128)} %get-tuple-element.33) | copy-start | bytes 1572868
  16.3 11.8 %copy-start.8 = (f32[2,256,256]{2,1,0:T(8,128)S(1)}, f32[2,256,256]{2,1,0:T(8,128)}, u32[]{:S(2)}) copy-start(f32[2,256,256]{2,1,0:T(8,128)} %get-tuple-element.25) | copy-start | bytes 1572868
  20.1 2.0 %copy-start.4 = (f32[8,2,256,256]{3,2,1,0:T(8,128)}, f32[8,2,256,256]{3,2,1,0:T(8,128)S(1)}, u32[]{:S(2)}) copy-start(f32[8,2,256,256]{3,2,1,0:T(8,128)S(1)} %get-tuple-element.21.turned.turned_in) | copy-start | bytes 12582916
  22.1 19.1 %copy-start.5 = (f32[8,256,256]{2,1,0:T(8,128)}, f32[8,256,256]{2,1,0:T(8,128)S(1)}, u32[]{:S(2)}) copy-start(f32[8,256,256]{2,1,0:T(8,128)S(1)} %get-tuple-element.24.amp_in) | copy-start | bytes 6291460
  22.1 9.4 %collective-permute-start.4 = (f32[2,256,256]{2,1,0:T(8,128)S(1)}, f32[2,256,256]{2,1,0:T(8,128)S(1)}, u32[]{:S(2)}, u32[]{:S(2)}) collective-permute-start(f32[2,256,256]{2,1,0:T(8,128)S(1)} %collective-permute-done.1.down0.down0_one), channel_id=1, source_target_pairs={{1,0},{2,1},{3,2},{4,3},{5,4},{6,5},{7,6},{9,8},{10,9},{11,10},{12... | collective-permute-start | bytes 1572872 | tf_op jit(solution)/shard_map/ppermute | solution.py:516
  23.4 19.3 %collective-permute-start.2 = (f32[2,256,256]{2,1,0:T(8,128)S(1)}, f32[2,256,256]{2,1,0:T(8,128)S(1)}, u32[]{:S(2)}, u32[]{:S(2)}) collective-permute-start(f32[2,256,256]{2,1,0:T(8,128)S(1)} %copy-done.9), channel_id=1, source_target_pairs={{8,0},{16,8},{24,16},{32,24},{40,32},{48,40},{56,48},{64,56},{72,6... | collective-permute-start | bytes 1572872 | tf_op jit(solution)/shard_map/ppermute | solution.py:516
  28.2 24.7 %collective-permute-start.5 = (f32[2,256,256]{2,1,0:T(8,128)S(1)}, f32[2,256,256]{2,1,0:T(8,128)S(1)}, u32[]{:S(2)}, u32[]{:S(2)}) collective-permute-start(f32[2,256,256]{2,1,0:T(8,128)S(1)} %copy-done.8), channel_id=1, source_target_pairs={{8,0},{16,8},{24,16},{32,24},{40,32},{48,40},{56,48},{64,56},{72,6... | collective-permute-start | bytes 1572872 | tf_op jit(solution)/shard_map/ppermute | solution.py:516
  42.7 10.2 %collective-permute-start.6 = (f32[2,256,256]{2,1,0:T(8,128)S(1)}, f32[2,256,256]{2,1,0:T(8,128)S(1)}, u32[]{:S(2)}, u32[]{:S(2)}) collective-permute-start(f32[2,256,256]{2,1,0:T(8,128)S(1)} %collective-permute-done.2.down0_two), channel_id=1, source_target_pairs={{1,0},{2,1},{3,2},{4,3},{5,4},{6,5},{7,6},{9,8},{10,9},{11,10},{12... | collective-permute-start | bytes 1572872 | tf_op jit(solution)/shard_map/ppermute | solution.py:516
  68.4 52.3 %copy-start.7 = (f32[4,256,256]{2,1,0:T(8,128)S(1)}, f32[4,256,256]{2,1,0:T(8,128)}, u32[]{:S(2)}) copy-start(f32[4,256,256]{2,1,0:T(8,128)} %get-tuple-element.28) | copy-start | bytes 3145732
  68.4 52.3 %collective-permute-start.8 = (f32[4,256,256]{2,1,0:T(8,128)}, f32[4,256,256]{2,1,0:T(8,128)S(1)}, u32[]{:S(2)}, u32[]{:S(2)}) collective-permute-start(f32[4,256,256]{2,1,0:T(8,128)} %get-tuple-element.29), channel_id=1, source_target_pairs={{0,1},{1,2},{2,3},{3,4},{4,5},{5,6},{6,7},{8,9},{9,10},{10,11},{11... | collective-permute-start | bytes 3145736 | tf_op jit(solution)/shard_map/ppermute | solution.py:516
  104.5 6.2 %collective-permute-start.11 = (f32[64,256]{1,0:T(8,128)S(1)}, f32[64,256]{1,0:T(8,128)S(1)}, u32[]{:S(2)}, u32[]{:S(2)}) collective-permute-start(f32[64,256]{1,0:T(8,128)S(1)} %reduce_sum.9), channel_id=1, source_target_pairs={{0,96},{8,104},{16,112},{24,120},{32,0},{40,8},{48,16},{56,24},{64... | collective-permute-start | bytes 196616 | tf_op jit(solution)/shard_map/ppermute | solution.py:531
  110.7 5.5 %collective-permute-start.12 = (f32[64,256]{1,0:T(8,128)S(1)}, f32[64,256]{1,0:T(8,128)S(1)}, u32[]{:S(2)}, u32[]{:S(2)}) collective-permute-start(f32[64,256]{1,0:T(8,128)S(1)} %collective-permute-done.11), channel_id=1, source_target_pairs={{0,96},{8,104},{16,112},{24,120},{32,0},{40,8},{48,16},{56,24},{64... | collective-permute-start | bytes 196616 | tf_op jit(solution)/shard_map/ppermute | solution.py:532
  116.2 6.8 %collective-permute-start.13 = (f32[64,256]{1,0:T(8,128)S(1)}, f32[64,256]{1,0:T(8,128)S(1)}, u32[]{:S(2)}, u32[]{:S(2)}) collective-permute-start(f32[64,256]{1,0:T(8,128)S(1)} %collective-permute-done.12), channel_id=1, source_target_pairs={{0,96},{8,104},{16,112},{24,120},{32,0},{40,8},{48,16},{56,24},{64... | collective-permute-start | bytes 196616 | tf_op jit(solution)/shard_map/ppermute | solution.py:533
  116.2 33.1 %collective-permute-start.7 = (f32[4,256,256]{2,1,0:T(8,128)}, f32[4,256,256]{2,1,0:T(8,128)S(1)}, u32[]{:S(2)}, u32[]{:S(2)}) collective-permute-start(f32[4,256,256]{2,1,0:T(8,128)} %get-tuple-element.27), channel_id=1, source_target_pairs={{0,1},{1,2},{2,3},{3,4},{4,5},{5,6},{6,7},{8,9},{9,10},{10,11},{11... | collective-permute-start | bytes 3145736 | tf_op jit(solution)/shard_map/ppermute | solution.py:516
  117.5 31.7 %collective-permute-start.10 = (f32[4,256,256]{2,1,0:T(8,128)}, f32[4,256,256]{2,1,0:T(8,128)S(1)}, u32[]{:S(2)}, u32[]{:S(2)}) collective-permute-start(f32[4,256,256]{2,1,0:T(8,128)} %get-tuple-element.30), channel_id=1, source_target_pairs={{0,8},{8,16},{16,24},{24,32},{32,40},{40,48},{48,56},{56,64},{64,7... | collective-permute-start | bytes 3145736 | tf_op jit(solution)/shard_map/ppermute | solution.py:516
  120.7 48.0 %copy-start = (f32[4,256,512]{2,1,0:T(8,128)S(1)}, f32[4,256,512]{2,1,0:T(8,128)}, u32[]{:S(2)}) copy-start(f32[4,256,512]{2,1,0:T(8,128)} %get-tuple-element.26.base) | copy-start | bytes 6291460
  120.9 47.8 %collective-permute-start.9 = (f32[4,256,256]{2,1,0:T(8,128)S(1)}, f32[4,256,256]{2,1,0:T(8,128)S(1)}, u32[]{:S(2)}, u32[]{:S(2)}) collective-permute-start(f32[4,256,256]{2,1,0:T(8,128)S(1)} %add.21), channel_id=1, source_target_pairs={{0,8},{8,16},{16,24},{24,32},{32,40},{40,48},{48,56},{56,64},{64,7... | collective-permute-start | bytes 3145736 | tf_op jit(solution)/shard_map/ppermute | solution.py:516
  122.9 4.3 %collective-permute-start.14 = (f32[64,256]{1,0:T(8,128)S(1)}, f32[64,256]{1,0:T(8,128)S(1)}, u32[]{:S(2)}, u32[]{:S(2)}) collective-permute-start(f32[64,256]{1,0:T(8,128)S(1)} %add_add_fusion.1), channel_id=1, source_target_pairs={{0,24},{8,0},{16,8},{24,16},{32,56},{40,32},{48,40},{56,48},{64,88... | collective-permute-start | bytes 196616 | tf_op jit(solution)/shard_map/ppermute | solution.py:531
  127.3 4.3 %collective-permute-start.15 = (f32[64,256]{1,0:T(8,128)S(1)}, f32[64,256]{1,0:T(8,128)S(1)}, u32[]{:S(2)}, u32[]{:S(2)}) collective-permute-start(f32[64,256]{1,0:T(8,128)S(1)} %collective-permute-done.14), channel_id=1, source_target_pairs={{0,24},{8,0},{16,8},{24,16},{32,56},{40,32},{48,40},{56,48},{64,88... | collective-permute-start | bytes 196616 | tf_op jit(solution)/shard_map/ppermute | solution.py:532
  131.6 4.3 %collective-permute-start.16 = (f32[64,256]{1,0:T(8,128)S(1)}, f32[64,256]{1,0:T(8,128)S(1)}, u32[]{:S(2)}, u32[]{:S(2)}) collective-permute-start(f32[64,256]{1,0:T(8,128)S(1)} %collective-permute-done.15), channel_id=1, source_target_pairs={{0,24},{8,0},{16,8},{24,16},{32,56},{40,32},{48,40},{56,48},{64,88... | collective-permute-start | bytes 196616 | tf_op jit(solution)/shard_map/ppermute | solution.py:533
